TPU v7x, 128 devices: a whole 4x4x4 slice. The times are simulated.
128 devices in a mesh: tp: 8 (over x, core), ep: 16 (over z, y).
Axes of the slice: x: 4, y: 4, z: 4, core: 2. Of those that a mesh axis runs over, the one named last changes fastest.
Arguments:
- hidden: bfloat16 [256, 7168], P(('tp', 'ep')), may hold values from -6 to 6
- queries: bfloat16 [256, 128, 576], P(('tp', 'ep')), may hold values from -1024 to 1024
- cache: bfloat16 [256, 1024, 576], P(('tp', 'ep')), may hold values from -6 to 6
- new_latent: bfloat16 [256, 576], P(('tp', 'ep')), may hold values from -6 to 6
- lengths: int32 [256], P(('tp', 'ep')), may hold values from 1 to 1024, 131072 in all
- w_values: bfloat16 [128, 512, 128], P('tp'), may hold values from -0.25 to 0.25
- w_out: bfloat16 [128, 128, 7168], P('tp', None, 'ep'), may hold values from -0.1875 to 0.1875
- gain_attn: float32 [7168], replicated, may hold values from 0.1 to 1.9
- w_dense_gate: bfloat16 [7168, 18432], P(None, ('tp', 'ep')), may hold values from -0.0625 to 0.0625
- w_dense_up: bfloat16 [7168, 18432], P(None, ('tp', 'ep')), may hold values from -0.0625 to 0.0625
- w_dense_down: bfloat16 [18432, 7168], P(('tp', 'ep')), may hold values from -0.046875 to 0.046875
- gain_moe: float32 [7168], replicated, may hold values from 0.1 to 1.9
- w_router: bfloat16 [7168, 16], replicated, may hold values from -0.0625 to 0.0625
- expert_ids: int32 [256, 8], P(('tp', 'ep')), may hold values from 0 to 15, all different within a row; in each aligned block of 2 rows (0 to 1, 2 to 3, ...) at most 2 rows name the same one
- w_expert_gate: bfloat16 [16, 7168, 2048], P('ep', None, 'tp'), may hold values from -0.0625 to 0.0625
- w_expert_up: bfloat16 [16, 7168, 2048], P('ep', None, 'tp'), may hold values from -0.0625 to 0.0625
- w_expert_down: bfloat16 [16, 2048, 7168], P('ep', 'tp'), may hold values from -0.125 to 0.125
Outputs:
- layer_out: bfloat16 [256, 7168], P(('tp', 'ep'))
Inputs may be any that keep to these rules, and one draw needn't show every extreme that they name: Request t attends to its first lengths[t] cached positions and to its new position. `expert_ids`: each row names 8 different experts; in the rows of one device no expert is named by more than 2 rows.
All inputs are finite; a program needn't handle non-finite values. No bound on the sum of `lengths` on one device may be relied on, other than what follows from the above.
Results may differ from a plain program's by a relative error of at most 0.022.
Values may be sent and summed in bfloat16 or wider, within the bound.
A program may use at most 128 MiB of HBM per device.

v0:
```python
import jax
import jax.numpy as jnp
from jax import lax
from jax.sharding import PartitionSpec as P

ROPE = 64
VD = 128


EPSILON = 1e-06
ROUTE_SCALE = 2.5


def rms_scale(values, norm_gain):
    mean_square = jnp.mean(values * values, axis=-1, keepdims=True)
    return values * lax.rsqrt(mean_square + EPSILON) * norm_gain


def latent_attention(queries, cache, new_latent, lengths, latent_dim):
    score_scale = (VD + ROPE) ** (-0.5)
    scores = (
        jnp.einsum("thc,tlc->thl", queries, cache, preferred_element_type=jnp.float32) * score_scale
    )
    own_score = (
        jnp.einsum("thc,tc->th", queries, new_latent, preferred_element_type=jnp.float32)
        * score_scale
    )
    places = jnp.arange(cache.shape[1], dtype=jnp.int32)
    in_range = places[None, None, :] < lengths[:, None, None]
    scores = jnp.where(in_range, scores, -jnp.inf)
    peak = jnp.maximum(jnp.max(scores, axis=2), own_score)
    weights = jnp.exp(scores - peak[:, :, None])
    own_weight = jnp.exp(own_score - peak)
    sum_total = jnp.sum(weights, axis=2) + own_weight
    probability = (weights / sum_total[:, :, None]).astype(jnp.bfloat16)
    own_probability = (own_weight / sum_total).astype(jnp.bfloat16)
    context = jnp.einsum(
        "thl,tlc->thc", probability, cache[:, :, :latent_dim], preferred_element_type=jnp.float32
    )
    context = context + own_probability.astype(jnp.float32)[:, :, None] * new_latent[
        :, None, :latent_dim
    ].astype(jnp.float32)
    return context.astype(jnp.bfloat16)


def body(
    hidden,
    queries,
    cache,
    new_latent,
    lengths,
    w_values,
    w_out,
    gain_attn,
    w_dense_gate,
    w_dense_up,
    w_dense_down,
    gain_moe,
    w_router,
    expert_ids,
    w_expert_gate,
    w_expert_up,
    w_expert_down,
):
    tok_rows = hidden.shape[0]
    feature_count = hidden.shape[1]
    latent_dim = w_values.shape[1]
    tp_count = lax.axis_size("tp")
    ep_count = lax.axis_size("ep")
    context = latent_attention(queries, cache, new_latent, lengths, latent_dim)
    grouped = lax.all_to_all(context, "tp", split_axis=1, concat_axis=0, tiled=True)
    head_values = jnp.einsum(
        "thl,hlv->thv", grouped, w_values, preferred_element_type=jnp.float32
    ).astype(jnp.bfloat16)
    head_values = head_values.reshape(grouped.shape[0], -1)
    out_columns = w_out.reshape(-1, w_out.shape[2])
    partial_value = jnp.dot(
        lax.all_gather(head_values, "ep", axis=0, tiled=True),
        out_columns,
        preferred_element_type=jnp.float32,
    )
    partial_value = partial_value.reshape(ep_count, tp_count, tok_rows, out_columns.shape[1])
    summed = lax.psum_scatter(
        partial_value.astype(jnp.bfloat16), "tp", scatter_dimension=1, tiled=True
    ).astype(jnp.float32)
    returned = lax.all_to_all(
        summed.astype(jnp.bfloat16), "ep", split_axis=0, concat_axis=3, tiled=True
    ).astype(summed.dtype)
    attention = returned.reshape(tok_rows, feature_count)
    after_attn = hidden.astype(jnp.float32) + attention
    normed = rms_scale(after_attn, gain_attn).astype(jnp.bfloat16)
    everyone = lax.all_gather(normed, ("tp", "ep"), axis=0, tiled=True)
    gate_part = jnp.dot(everyone, w_dense_gate, preferred_element_type=jnp.float32)
    up_part = jnp.dot(everyone, w_dense_up, preferred_element_type=jnp.float32)
    dense_act = (jax.nn.silu(gate_part) * up_part).astype(jnp.bfloat16)
    dense_out = lax.psum_scatter(
        jnp.dot(dense_act, w_dense_down, preferred_element_type=jnp.float32),
        ("tp", "ep"),
        scatter_dimension=0,
        tiled=True,
    )
    second = after_attn + dense_out
    routed_in = rms_scale(second, gain_moe).astype(jnp.bfloat16)
    affinity = jax.nn.sigmoid(jnp.dot(routed_in, w_router, preferred_element_type=jnp.float32))
    expert_count = w_router.shape[1]
    top_count = expert_ids.shape[1]
    choose = expert_ids[:, :, None] == jnp.arange(expert_count, dtype=jnp.int32)[None, None, :]
    picked = jnp.sum(jnp.where(choose, affinity[:, None, :], 0.0), axis=2)
    route_weight = ROUTE_SCALE * picked / jnp.sum(picked, axis=1, keepdims=True)
    flat_choose = choose.reshape(tok_rows * top_count, expert_count).astype(jnp.int32)
    earlier = jnp.cumsum(flat_choose, axis=0) - flat_choose
    slot_index = jnp.sum(earlier * flat_choose, axis=1)
    target = expert_ids.reshape(-1) * tok_rows + slot_index
    place_mask = (
        target[:, None] == jnp.arange(expert_count * tok_rows, dtype=jnp.int32)[None, :]
    ).astype(jnp.float32)
    row_owner = jnp.arange(tok_rows * top_count, dtype=jnp.int32) // top_count
    owner_mask = (row_owner[:, None] == jnp.arange(tok_rows, dtype=jnp.int32)[None, :]).astype(
        jnp.float32
    )
    dispatch = jnp.dot(place_mask.T, owner_mask, precision=lax.Precision.HIGHEST)
    outgoing = jnp.dot(
        dispatch.astype(jnp.bfloat16), routed_in, preferred_element_type=jnp.float32
    ).astype(jnp.bfloat16)
    outgoing = outgoing.reshape(expert_count, tok_rows, feature_count)
    arrived = lax.all_to_all(outgoing, "ep", split_axis=0, concat_axis=1, tiled=True)
    group_slots = lax.all_gather(arrived, "tp", axis=1, tiled=True)
    gate_rows = jnp.einsum(
        "esd,edh->esh", group_slots, w_expert_gate, preferred_element_type=jnp.float32
    )
    up_rows = jnp.einsum(
        "esd,edh->esh", group_slots, w_expert_up, preferred_element_type=jnp.float32
    )
    activated = (jax.nn.silu(gate_rows) * up_rows).astype(jnp.bfloat16)
    partial_out = jnp.einsum(
        "esh,ehd->esd", activated, w_expert_down, preferred_element_type=jnp.float32
    )
    expert_out = lax.psum_scatter(
        partial_out.astype(jnp.bfloat16), "tp", scatter_dimension=1, tiled=True
    )
    returned_rows = lax.all_to_all(expert_out, "ep", split_axis=1, concat_axis=0, tiled=True)
    combine = jnp.dot(
        (owner_mask * route_weight.reshape(-1)[:, None]).T,
        place_mask,
        precision=lax.Precision.HIGHEST,
    )
    routed_sum = jnp.dot(
        combine,
        returned_rows.reshape(expert_count * tok_rows, feature_count).astype(jnp.float32),
        precision=lax.Precision.HIGHEST,
    )
    return (second + routed_sum).astype(jnp.bfloat16)


def solution(mesh):
    in_specs = (
        P(("tp", "ep"), None),
        P(("tp", "ep"), None, None),
        P(("tp", "ep"), None, None),
        P(("tp", "ep"), None),
        P(("tp", "ep")),
        P("tp", None, None),
        P("tp", None, "ep"),
        P(),
        P(None, ("tp", "ep")),
        P(None, ("tp", "ep")),
        P(("tp", "ep"), None),
        P(),
        P(),
        P(("tp", "ep"), None),
        P("ep", None, "tp"),
        P("ep", None, "tp"),
        P("ep", "tp", None),
    )
    out_specs = P(("tp", "ep"), None)
    return jax.shard_map(body, mesh=mesh, in_specs=in_specs, out_specs=out_specs, check_vma=False)
```

profile of v0, /device:TPU:0, one launch (start us, length us, event | category | flops | bytes accessed | tf_op | source)
XLA Modules:
  0.0 490.8 jit_solution(17889498009085144191)
XLA Ops:
  8.2 1.1 fusion.65
  9.3 2.5 fusion.78
  13.4 11.7 %all_to_all.48 = bf16[2,128,512]{2,0,1:T(2,128)(2,1)S(1)} all-to-all(bf16[2,128,512]{2,0,1:T(2,128)(2,1)S(1)} %copy.47), channel_id=1, replica_groups=mesh['tp'=8,'ep'=16] {'tp'}, dimensions={1} | all-to-all | bytes 524288 | tf_op jit(solution)/shard_map/all_to_all | solution.py:71
  26.6 2.7 copy.50
  29.2 1.8 reshape.159
  31.0 39.1 %all-gather.5.cloned.1.call-done = bf16[256,2048]{1,0:T(8,128)(2,1)} async-done(((bf16[16,2048]{1,0:T(8,128)(2,1)}), bf16[256,2048]{1,0:T(8,128)(2,1)}) %all-gather.5.cloned.1.call-update) | async-done | bytes 1048592 | tf_op jit(solution)/shard_map/all_gather | solution.py:78
  70.1 1.7 dot_general.54
  71.9 2.2 fusion.20
  75.0 29.8 %reduce-scatter.3.cloned.1.call-done = bf16[16,1,2,448]{3,0,2,1:T(8,128)(2,1)} async-done(((bf16[16,8,2,448]{3,0,2,1:T(8,128)(2,1)}), bf16[16,1,2,448]{3,0,2,1:T(8,128)(2,1)}) %reduce-scatter.3.cloned.1.call-update) | async-done | bytes 28688 | tf_op jit(solution)/shard_map/reduce_scatter | solution.py:83
  105.6 14.4 %all_to_all.49 = bf16[16,1,2,448]{3,2,1,0:T(2,128)(2,1)S(1)} all-to-all(bf16[16,1,2,448]{3,2,1,0:T(2,128)(2,1)S(1)} %copy.53), channel_id=1, replica_groups=mesh['tp'=8,'ep'=16] {'ep'}, dimensions={0} | all-to-all | bytes 57344 | tf_op jit(solution)/shard_map/all_to_all | solution.py:86
  121.1 61.6 %all-gather.9.cloned.1.call-done = bf16[128,2,7168]{2,1,0:T(2,128)(2,1)} async-done(((bf16[1,2,7168]{2,1,0:T(2,128)(2,1)}), bf16[128,2,7168]{2,1,0:T(2,128)(2,1)}) %all-gather.9.cloned.1.call-update) | async-done | bytes 3670032 | tf_op jit(solution)/shard_map/all_gather | solution.py:92
  182.7 8.4 %reshape.156 = bf16[256,7168]{1,0:T(8,128)(2,1)} reshape(bf16[128,2,7168]{2,1,0:T(2,128)(2,1)} %all-gather.9.cloned.1.call-done) | data formatting | bytes 7340032
  191.1 3.4 fusion.79
  194.5 10.5 %fusion.34 = f32[256,7168]{1,0:T(8,128)} fusion(bf16[144,7168]{1,0:T(8,128)(2,1)} %param.27, bf16[256,7168]{1,0:T(8,128)(2,1)} %reshape.156, bf16[7168,144]{0,1:T(8,128)(2,1)} %param.26, f32[256,144]{0,1:T(8,128)S(1)} %fusion.79), kind=kOutput, calls=%fused_computation.26 | convolution fusion | flops 1057185792 | bytes 15286272 | tf_op jit(solution)/shard_map/dot_general | solution.py:97
  206.3 156.3 %all-reduce.3.cloned.1.call-done = f32[256,7168]{1,0:T(8,128)} async-done(((f32[256,7168]{1,0:T(8,128)}), f32[256,7168]{1,0:T(8,128)}) %all-reduce.3.cloned.1.call-update) | async-done | bytes 7340048
  364.2 15.7 %all_to_all.50 = bf16[16,2,7168]{2,1,0:T(2,128)(2,1)S(1)} all-to-all(bf16[16,2,7168]{2,1,0:T(2,128)(2,1)S(1)} %reshape.147), channel_id=1, replica_groups=mesh['tp'=8,'ep'=16] {'ep'}, dimensions={0} | all-to-all | bytes 917504 | tf_op jit(solution)/shard_map/all_to_all | solution.py:126
  380.9 27.2 %all-gather.7.cloned.1.call-done = bf16[1,256,7168]{2,1,0:T(8,128)(2,1)} async-done(((bf16[1,32,7168]{2,1,0:T(8,128)(2,1)}), bf16[1,256,7168]{2,1,0:T(8,128)(2,1)}) %all-gather.7.cloned.1.call-update) | async-done | bytes 3670032 | tf_op jit(solution)/shard_map/all_gather | solution.py:127
  408.1 4.3 fusion.5
  412.4 10.0 %fusion = bf16[1,256,7168]{2,1,0:T(8,128)(2,1)} fusion(bf16[1,256,7168]{2,1,0:T(8,128)(2,1)} %param.33, bf16[1,7168,256]{2,1,0:T(8,128)(2,1)} %param.32, bf16[1,256,7168]{2,1,0:T(8,128)(2,1)} %all-gather.7.cloned.1.call-done, f32[256,256]{1,0:T(8,128)S(1)} %fusion.5), kind=kOutput, calls=%fused_computation.1 | convolution fusion | flops 1881276416 | bytes 14942208 | tf_op jit(solution)/shard_map/esh,ehd->esd/dot_general | solution.py:135
  423.8 35.5 %reduce-scatter.5.cloned.1.call-done = bf16[1,32,7168]{2,1,0:T(8,128)(2,1)} async-done(((bf16[1,256,7168]{2,1,0:T(8,128)(2,1)}), bf16[1,32,7168]{2,1,0:T(8,128)(2,1)}) %reduce-scatter.5.cloned.1.call-update) | async-done | bytes 458768 | tf_op jit(solution)/shard_map/reduce_scatter | solution.py:138
  459.3 1.7 copy.75
  461.5 3.4 reduce.1
  465.9 7.0 %all-to-all-start.3 = ((bf16[16,2,7168]{2,1,0:T(2,128)(2,1)}), bf16[16,2,7168]{2,1,0:T(2,128)(2,1)S(1)}, u32[]{:S(2)}, u32[]{:S(2)}) async-start(bf16[16,2,7168]{2,1,0:T(2,128)(2,1)} %reshape.161), calls=%async_computation.5 | async-start | bytes 917504 | tf_op jit(solution)/shard_map/all_to_all | solution.py:141
  473.3 9.3 %all-to-all-done.3 = bf16[16,2,7168]{2,1,0:T(2,128)(2,1)S(1)} async-done(((bf16[16,2,7168]{2,1,0:T(2,128)(2,1)}), bf16[16,2,7168]{2,1,0:T(2,128)(2,1)S(1)}, u32[]{:S(2)}, u32[]{:S(2)}) %all-to-all-start.3) | async-done | bytes 458784 | tf_op jit(solution)/shard_map/all_to_all | solution.py:141
  (69 shorter events, 15.9 us)
Async XLA Ops:
  6.5 18.9 %copy-start = (bf16[16,512,128]{2,1,0:T(8,128)(2,1)S(1)}, bf16[16,512,128]{2,1,0:T(8,128)(2,1)}, u32[]{:S(2)}) copy-start(bf16[16,512,128]{2,1,0:T(8,128)(2,1)} %param.22) | copy-start | bytes 6291460
  6.5 63.5 %all-gather.5.cloned.1.call-start = ((), (), s32[]{:S(2)}) async-start(), calls=%async_computation.6 | async-start | bytes 1114112 | tf_op jit(solution)/shard_map/all_gather | solution.py:78
  6.5 5.7 %copy-start.2 = (bf16[2,1024,576]{1,2,0:T(8,128)(2,1)S(1)}, bf16[2,1024,576]{1,2,0:T(8,128)(2,1)}, u32[]{:S(2)}) copy-start(bf16[2,1024,576]{1,2,0:T(8,128)(2,1)} %param.19) | copy-start | bytes 7077892
  26.5 78.3 %reduce-scatter.3.cloned.1.call-start = ((), (), s32[]{:S(2)}) async-start(), calls=%async_computation.7 | async-start | bytes 294912 | tf_op jit(solution)/shard_map/reduce_scatter | solution.py:83
  71.8 48.3 %copy-start.4 = (bf16[2,7168]{1,0:T(2,128)(2,1)S(1)}, bf16[2,7168]{1,0:T(2,128)(2,1)}, u32[]{:S(2)}) copy-start(bf16[2,7168]{1,0:T(2,128)(2,1)} %param.17) | copy-start | bytes 86020
  71.8 48.5 %copy-start.5 = (f32[7168]{0:T(1024)S(1)}, f32[7168]{0:T(1024)}, u32[]{:S(2)}) copy-start(f32[7168]{0:T(1024)} %param.24) | copy-start | bytes 86020
  75.0 107.7 %all-gather.9.cloned.1.call-start = ((), (), s32[]{:S(2)}) async-start(), calls=%async_computation.10 | async-start | bytes 3698688 | tf_op jit(solution)/shard_map/all_gather | solution.py:92
  121.1 70.0 %copy-start.3 = (bf16[7168,144]{0,1:T(8,128)(2,1)S(1)}, bf16[7168,144]{0,1:T(8,128)(2,1)}, u32[]{:S(2)}) copy-start(bf16[7168,144]{0,1:T(8,128)(2,1)} %param.25) | copy-start | bytes 6193156
  121.1 241.5 %all-reduce.3.cloned.1.call-start = ((), (), s32[]{:S(2)}) async-start(), calls=%async_computation.11 | async-start | bytes 14680064
  205.0 0.7 copy-start.7
  205.0 158.7 %copy-start.6 = (f32[7168]{0:T(1024)S(1)}, f32[7168]{0:T(1024)}, u32[]{:S(2)}) copy-start(f32[7168]{0:T(1024)} %param.28) | copy-start | bytes 86020
  205.0 203.1 %all-gather.7.cloned.1.call-start = ((), (), s32[]{:S(2)}) async-start(), calls=%async_computation.8 | async-start | bytes 4128768 | tf_op jit(solution)/shard_map/all_gather | solution.py:127
  380.9 78.4 %reduce-scatter.5.cloned.1.call-start = ((), (), s32[]{:S(2)}) async-start(), calls=%async_computation.9 | async-start | bytes 4128768 | tf_op jit(solution)/shard_map/reduce_scatter | solution.py:138
  422.4 0.9 copy-start.8
  423.3 60.6 %copy-start.1 = (bf16[16,512,128]{2,1,0:T(8,128)(2,1)S(1)}, bf16[16,512,128]{2,1,0:T(8,128)(2,1)}, u32[]{:S(2)}) copy-start(bf16[16,512,128]{2,1,0:T(8,128)(2,1)} %param.22) | copy-start | bytes 6291460
  465.9 16.7 %all-to-all-start.3 = ((bf16[16,2,7168]{2,1,0:T(2,128)(2,1)}), bf16[16,2,7168]{2,1,0:T(2,128)(2,1)S(1)}, u32[]{:S(2)}, u32[]{:S(2)}) async-start(bf16[16,2,7168]{2,1,0:T(2,128)(2,1)} %reshape.161), calls=%async_computation.5 | async-start | bytes 917504 | tf_op jit(solution)/shard_map/all_to_all | solution.py:141
Sparse Core Ops, SparseCore 0:
  26.6 43.4 all-gather.4
  75.1 29.6 reduce-scatter.2
  121.2 61.4 all-gather.8
  205.1 157.4 all-reduce.2
  381.0 27.0 all-gather.6
  422.5 36.7 reduce-scatter.4
where the time goes:
time: 492 us; the launch traced here: 491 us
  waiting for transfers between devices  359 us (73%)
  blocking collectives  41.8 us (8%)
  matrix products  37.4 us (8%)
  local copies, waits for them, and re-layouts  23.8 us (5%)
  between operations  13.7 us (3%)
  other arithmetic  7.97 us (2%)
  starting transfers between devices  7.37 us (1%)
    unnamed x7, waiting for transfers between devices  156 us
    all_gather x1, waiting for transfers between devices, body(): everyone = lax.all_gather(normed, ('tp', 'ep'), axis=0, tiled=True)  61.6 us
    all_gather x1, waiting for transfers between devices, body(): lax.all_gather(head_values, 'ep', axis=0, tiled=True)  39.1 us
    reduce_scatter x1, waiting for transfers between devices, body(): lax.psum_scatter(partial_out.astype(jnp.bfloat16), 'tp', scatter_dimensio...  35.5 us
    reduce_scatter x1, waiting for transfers between devices, body(): lax.psum_scatter(partial_value.astype(jnp.bfloat16), 'tp', scatter_dimens...  29.8 us
    all_gather x1, waiting for transfers between devices, body(): group_slots = lax.all_gather(arrived, 'tp', axis=1, tiled=True)  27.2 us
    all_to_all x1, blocking collectives, body(): lax.all_to_all(outgoing, 'ep', split_axis=0, concat_axis=1, tiled=True)  15.7 us
    all_to_all x1, blocking collectives, body(): lax.all_to_all(summed.astype(jnp.bfloat16), 'ep', split_axis=0, concat_ax...  14.4 us
  transfers between devices with their start and end apart: 7, of which 7 were waited for; matrix products, arithmetic and copies ran while one was open for 1% of the time, Pallas kernels for 0%

commit v1 on v0

v1 whole, which is shorter than its diff:
```python
import functools

import jax
import jax.numpy as jnp
from jax import lax
from jax.experimental import pallas as pl
from jax.experimental.pallas import tpu as pltpu
from jax.sharding import PartitionSpec as P

ROPE = 64
VD = 128
D = 7168
BLK = 896
EPSILON = 1e-06
ROUTE_SCALE = 2.5
MESH = pl.DeviceIdType.MESH
F32 = jnp.float32
BF16 = jnp.bfloat16
VMEM_LIMIT = 60 * 2**20


PORTIONS = ((0, 384, ("x", "y", "z")), (384, 256, ("y", "z", "x")), (640, 256, ("z", "x", "y")))
DIMS = ("z", "y", "x")


def coords():
    tp, ep = lax.axis_index("tp"), lax.axis_index("ep")
    return dict(x=tp // 2, c=tp % 2, z=ep // 4, y=ep % 4)


def device(at):
    return (at["x"] * 2 + at["c"], at["z"] * 4 + at["y"])


def moved(at, **steps):
    new = dict(at)
    for name, step in steps.items():
        new[name] = lax.rem(at[name] + step, 2 if name == "c" else 4)
    return new


def meet(partners):
    barrier = pltpu.get_barrier_semaphore()
    for partner in partners:
        pl.semaphore_signal(barrier, inc=1, device_id=device(partner), device_id_type=MESH)
    pl.semaphore_wait(barrier, len(partners))


def remote(src, dst, send, recv, partner):
    return pltpu.make_async_remote_copy(
        src_ref=src, dst_ref=dst, send_sem=send, recv_sem=recv, device_id=device(partner), device_id_type=MESH
    )


def dot_nt(a, b):
    return lax.dot_general(a, b, (((1,), (1,)), ((), ())), preferred_element_type=F32)


def dot(a, b):
    return jnp.dot(a, b, preferred_element_type=F32)


def attn_kernel(
    ctx_ref, hid_ref, wv_hbm, wo_hbm, out_ref,
    wv, wo, ctx_in, heads, part, part_in, hid_out, hid_in, load_sem,
    hid_s, hid_r, ctx_s, ctx_r, hv_s, hv_r, part_s, part_r,
):
    me = coords()
    x, c, z, y = me["x"], me["c"], me["z"], me["y"]
    yh, yl = y // 2, y % 2
    tp = x * 2 + c
    pad = pl.multiple_of(yl * 64, 64)
    load_wv = pltpu.make_async_copy(wv_hbm, wv, load_sem.at[0])
    load_wo = pltpu.make_async_copy(wo_hbm, wo.at[:, pl.ds(pad, 448), :], load_sem.at[1])
    load_wv.start()
    load_wo.start()
    wo[:, pl.ds(pl.multiple_of((1 - yl) * 448, 64), 64), :] = jnp.zeros((16, 64, 128), BF16)

    def at_tp(step):
        other = lax.rem(tp + step, 8)
        return dict(me, x=other // 2, c=other % 2)

    tp_steps = [(dt, dy) for dy in (0, 1) for dt in range(8) if dt or dy]
    part_to = [dict(at_tp(dt), y=yh * 2 + (yl + dy) % 2) for dt, dy in tp_steps]
    hid_steps = [(dz, dy) for dy in (0, 2) for dz in range(4) if dz or dy]
    hid_to = [moved(me, z=dz, y=dy) for dz, dy in hid_steps]
    other_odd = dict(me, y=lax.rem(yh * 2 + 2, 4) + (1 - yl))
    meet(part_to + hid_to + [other_odd])

    first = (z * 2 + yh) * 2
    row = lax.broadcasted_iota(jnp.int32, (16, BLK), 0)
    for f in range(8):
        both = hid_ref[:, f * BLK : (f + 1) * BLK].astype(F32)
        placed = jnp.where(row == first, both[0:1, :], jnp.where(row == first + 1, both[1:2, :], 0.0))
        hid_out[f // 2, f % 2] = placed.astype(BF16)
    copies = []
    ctx_copies = []
    for step in range(1, 8):
        to = at_tp(step)
        copy = remote(ctx_ref.at[:, to["x"] * 2 + to["c"]], ctx_in.at[tp], ctx_s.at[step - 1], ctx_r.at[step - 1], to)
        copy.start()
        ctx_copies.append(copy)
    hid_copies = []
    for i, to in enumerate(hid_to):
        copy = remote(hid_out.at[to["z"], to["y"] // 2], hid_in.at[z, yh], hid_s.at[i], hid_r.at[i], to)
        copy.start()
        hid_copies.append(copy)
    ctx_in[tp] = ctx_ref[:, tp]
    hid_in[z, yh] = hid_out[z, yh]
    for copy in ctx_copies:
        copy.wait_recv()
    load_wv.wait()

    i = lax.broadcasted_iota(jnp.int32, (256, 256), 0)
    j = lax.broadcasted_iota(jnp.int32, (256, 256), 1)
    turn = ((i & 15) * 16 + (i >> 4) == j).astype(BF16)
    by_head = dot(turn, ctx_in[...].reshape(256, 512)).astype(BF16)
    for h in range(16):
        heads[z, y, :, h * 128 : (h + 1) * 128] = dot(by_head[h * 16 : (h + 1) * 16, :], wv[h]).astype(BF16)

    halves = ((0, "z", "y"), (1, "y", "z"))
    sends = []
    for half, one, two in halves:
        lanes = pl.ds(half * 1024, 1024)
        for step in range(1, 4):
            mine = heads.at[z, y, :, lanes]
            copy = remote(mine, mine, hv_s.at[half, 0, step - 1], hv_r.at[half, 0, step - 1], moved(me, **{one: step}))
            copy.start()
            sends.append(copy)
    for half, one, two in halves:
        lanes = pl.ds(half * 1024, 1024)
        for step in range(1, 4):
            sends[half * 3 + step - 1].wait_recv()
        for step in range(1, 4):
            slab = heads.at[:, y, :, lanes] if two == "y" else heads.at[z, :, :, lanes]
            copy = remote(slab, slab, hv_s.at[half, 1, step - 1], hv_r.at[half, 1, step - 1], moved(me, **{two: step}))
            copy.start()
            sends.append(copy)
    load_wo.wait()
    for copy in sends[6:]:
        copy.wait_recv()

    total = jnp.zeros((256, 512), F32)
    for pair in range(8):
        rows = heads[:, :, :, pair * 256 : (pair + 1) * 256].reshape(256, 256)
        weights = jnp.concatenate([wo[2 * pair], wo[2 * pair + 1]], axis=1)
        total = total + dot_nt(rows, weights)
    t, from_yh, from_z = i & 1, (i >> 1) & 1, (i >> 2) & 3
    source = from_z * 64 + (from_yh * 2 + (i >> 7)) * 16 + ((i >> 4) & 7) * 2 + t
    order = (source == j).astype(BF16)
    part[...] = dot(order, total.astype(BF16)).astype(BF16).reshape(2, 8, 16, 512)
    part_copies = []
    for i_to, to in enumerate(part_to):
        copy = remote(
            part.at[to["y"] % 2, to["x"] * 2 + to["c"]], part_in.at[yl, tp], part_s.at[i_to], part_r.at[i_to], to
        )
        copy.start()
        part_copies.append(copy)
    part_in[yl, tp] = part[yl, tp]
    for copy in hid_copies:
        copy.wait_recv()
    out_ref[...] = jnp.sum(hid_in[...].astype(F32), axis=(0, 1))
    for copy in part_copies:
        copy.wait_recv()
    sums = jnp.sum(part_in[...].astype(F32), axis=1)
    out_ref[:, 0:512] += sums[0]
    out_ref[:, 384:896] += sums[1]
    for copy in ctx_copies + hid_copies + sends + part_copies:
        copy.wait_send()


def attn_exchange(context, hidden, w_values, w_out):
    any_space = pl.BlockSpec(memory_space=pl.ANY)
    vmem = pl.BlockSpec(memory_space=pltpu.VMEM)
    dma = pltpu.SemaphoreType.DMA
    return pl.pallas_call(
        attn_kernel,
        out_shape=jax.ShapeDtypeStruct((16, BLK), F32),
        in_specs=[vmem, vmem, any_space, any_space],
        out_specs=vmem,
        scratch_shapes=[
            pltpu.VMEM((16, 512, 128), BF16),
            pltpu.VMEM((16, 512, 128), BF16),
            pltpu.VMEM((8, 2, 16, 512), BF16),
            pltpu.VMEM((4, 4, 16, 2048), BF16),
            pltpu.VMEM((2, 8, 16, 512), BF16),
            pltpu.VMEM((2, 8, 16, 512), BF16),
            pltpu.VMEM((4, 2, 16, BLK), BF16),
            pltpu.VMEM((4, 2, 16, BLK), BF16),
            dma((2,)),
            dma((7,)), dma((7,)), dma((7,)), dma((7,)),
            dma((2, 2, 3)), dma((2, 2, 3)), dma((15,)), dma((15,)),
        ],
        compiler_params=pltpu.CompilerParams(collective_id=0, has_side_effects=True, vmem_limit_bytes=VMEM_LIMIT),
        name="attn_exchange",
    )(context, hidden, w_values, w_out)


def gather_region(at, portion, phase):
    start, width, order = PORTIONS[portion]
    done = order[::-1][:phase]
    index = tuple(pl.ds(0, 4) if name in done else at[name] for name in DIMS)
    return index + (at["c"], slice(None), pl.ds(start, width))


def ffn_kernel(routed, *refs):
    if routed:
        x_ref, gain_ref, wr_ref, ids_ref, wg_hbm, wu_hbm, wd_hbm, out_ref, *refs = refs
        own, final_in, final_s, final_r, *refs = refs
    else:
        x_ref, gain_ref, wg_hbm, wu_hbm, wd_hbm, out_ref, *refs = refs
    (
        wg, wu, wd, full, partial, core_in, acc, square, router_acc,
        in1a, in1b, in1c, b_a, b_b, b_c, in2a, in2b, in2c, c_a, c_b, c_c, in3a, in3b, in3c,
        load_sem, gather_s, gather_r, pair_s, pair_r, core_s, core_r, sum_s, sum_r,
    ) = refs
    in1, held2 = (in1a, in1b, in1c), (b_a, b_b, b_c)
    in2, held3 = (in2a, in2b, in2c), (c_a, c_b, c_c)
    in3 = (in3a, in3b, in3c)
    me = coords()
    z, y, x, c = me["z"], me["y"], me["x"], me["c"]
    yh, yl = y // 2, y % 2
    f_me = z * 2 + yh
    hidden = acc.shape[2]
    loads = [
        pltpu.make_async_copy(src, dst, load_sem.at[i])
        for i, (src, dst) in enumerate(((wg_hbm, wg), (wu_hbm, wu), (wd_hbm, wd)))
    ]
    for load in loads:
        load.start()
    sibling = moved(me, c=1)
    ring = {name: [moved(me, **{name: step}) for step in (1, 2, 3)] for name in DIMS}
    back = {name: [moved(me, **{name: 4 - step}) for step in (1, 2, 3)] for name in DIMS}
    partners = ring["x"] + ring["y"] + ring["z"] + [sibling]
    if routed:
        final_steps = [(dz, dy) for dy in (0, 2) for dz in range(4) if dz or dy]
        final_to = [moved(me, z=dz, y=dy) for dz, dy in final_steps]
        partners = partners + [moved(me, z=dz, y=2) for dz in (1, 2, 3)]
    full[z, y, x, c] = (x_ref[...] * gain_ref[pl.ds(f_me, 1), :]).astype(BF16)
    meet(partners)

    sends = []
    for phase in range(3):
        for p in range(3):
            axis = PORTIONS[p][2][2 - phase]
            if phase > 0:
                earlier = PORTIONS[p][2][3 - phase]
                for k in range(3):
                    region = full.at[gather_region(back[earlier][k], p, phase - 1)]
                    remote(
                        region, region, gather_s.at[p, phase - 1, k], gather_r.at[p, phase - 1, k], ring[earlier][k]
                    ).wait_recv()
            region = full.at[gather_region(me, p, phase)]
            for k in range(3):
                copy = remote(region, region, gather_s.at[p, phase, k], gather_r.at[p, phase, k], ring[axis][k])
                copy.start()
                sends.append(copy)
            if phase == 2:
                copy = remote(region, region, pair_s.at[p, 3], pair_r.at[p, 3], sibling)
                copy.start()
                sends.append(copy)
    for k in (0, 2, 1):
        for p in range(3):
            axis = PORTIONS[p][2][0]
            region = full.at[gather_region(back[axis][k], p, 2)]
            remote(region, region, gather_s.at[p, 2, k], gather_r.at[p, 2, k], ring[axis][k]).wait_recv()
            copy = remote(region, region, pair_s.at[p, k], pair_r.at[p, k], sibling)
            copy.start()
            sends.append(copy)
    for k in (3, 0, 2, 1):
        for p in range(3):
            axis = PORTIONS[p][2][0]
            place = dict(sibling) if k == 3 else dict(back[axis][k], c=sibling["c"])
            region = full.at[gather_region(place, p, 2)]
            remote(region, region, pair_s.at[p, k], pair_r.at[p, k], sibling).wait_recv()
    loads[0].wait()
    loads[1].wait()

    acc[...] = jnp.zeros_like(acc)
    square[...] = jnp.zeros_like(square)
    if routed:
        router_acc[...] = jnp.zeros_like(router_acc)

    def up_step(f, carry):
        rows = full[f // 2, pl.ds((f % 2) * 2, 2)].reshape(256, BLK)
        at = pl.ds(pl.multiple_of(f * BLK, 128), BLK)
        if routed:
            acc[0] += dot(rows, wg[at, :])
            acc[1] += dot(rows, wu[at, :])
            router_acc[...] += dot_nt(rows, wr_ref[:, at])
        else:
            acc[0] += dot_nt(rows, wg[:, at])
            acc[1] += dot_nt(rows, wu[:, at])
        gain = gain_ref[pl.ds(f, 1), :]
        plain = rows.astype(F32) * (1.0 / gain)
        plain = plain * plain
        piece = plain[:, 0:128]
        for k in range(1, 7):
            piece = piece + plain[:, k * 128 : (k + 1) * 128]
        square[...] += piece
        return carry

    lax.fori_loop(0, 8, up_step, 0)
    scale = lax.rsqrt(jnp.sum(square[...], axis=1, keepdims=True) * (1.0 / D) + EPSILON)
    gate = acc[0] * scale
    act = gate / (1.0 + jnp.exp(-gate)) * (acc[1] * scale)
    if routed:
        affinity = 1.0 / (1.0 + jnp.exp(-(router_acc[...] * scale)))
        lane = lax.broadcasted_iota(jnp.int32, (256, 16), 1)
        chosen = jnp.zeros((256, 16), F32)
        for k in range(ids_ref.shape[1]):
            chosen = chosen + jnp.where(ids_ref[:, k : k + 1] == lane, 1.0, 0.0)
        picked = jnp.where(chosen > 0.5, affinity, 0.0)
        below = jnp.sum(picked, axis=1, keepdims=True)
        mine = lane == z * 4 + y
        weight = ROUTE_SCALE * jnp.sum(jnp.where(mine, picked, 0.0), axis=1, keepdims=True) / below
        wanted = jnp.sum(jnp.where(mine, chosen, 0.0), axis=1, keepdims=True) > 0.5
        act = jnp.where(wanted, act * weight, 0.0)
    act = act.astype(BF16)
    loads[2].wait()

    core_copies = []

    def core_add(part):
        core_copies[part].wait_recv()

        def add(row, carry):
            both = partial[part, row, :, c].astype(F32) + core_in[part, row].astype(F32)
            partial[part, row, :, c] = both.astype(BF16)
            return carry

        lax.fori_loop(0, 4, add, 0)

    for part in range(4):
        for half in range(2):
            f = part * 2 + half
            block = dot(act, wd[:, f * BLK : (f + 1) * BLK])
            partial[part, half * 2 : half * 2 + 2] = block.astype(BF16).reshape(2, 4, 2, 16, BLK)
        copy = remote(
            partial.at[part, :, :, sibling["c"]], core_in.at[part], core_s.at[part], core_r.at[part], sibling
        )
        copy.start()
        core_copies.append(copy)
        if part:
            core_add(part - 1)
    core_add(3)

    def start(p, phase, source):
        axis = PORTIONS[p][2][phase]
        into = (in1, in2, in3)[phase][p]
        copies = []
        for k in range(3):
            copy = remote(source(ring[axis][k][axis]), into.at[k], sum_s.at[p, phase, k], sum_r.at[p, phase, k], ring[axis][k])
            copy.start()
            copies.append(copy)
        sends.extend(copies)
        return copies

    def cut(p, target):
        begin, width, order = PORTIONS[p]
        index = [slice(None)] * 3
        index[DIMS.index(order[0])] = target
        return tuple(index) + (c, slice(None), pl.ds(begin, width))

    flying = [start(p, 0, lambda target, p=p: partial.at[cut(p, target)]) for p in range(3)]
    next_flying = []
    for p in range(3):
        begin, width, order = PORTIONS[p]
        for copy in flying[p]:
            copy.wait_recv()

        def add(i, carry, p=p, begin=begin, width=width, order=order):
            left = [name for name in DIMS if name != order[0]]
            index = {order[0]: me[order[0]], left[0]: i, left[1]: slice(None)}
            index = tuple(index[name] for name in DIMS) + (c, slice(None), pl.ds(begin, width))
            value = partial[index].astype(F32)
            for k in range(3):
                value = value + in1[p][k, i].astype(F32)
            held2[p][i] = value.astype(BF16)
            return carry

        lax.fori_loop(0, 4, add, 0)
        left = [name for name in DIMS if name != order[0]]
        if order[1] == left[0]:
            next_flying.append(start(p, 1, lambda target, p=p: held2[p].at[target]))
        else:
            next_flying.append(start(p, 1, lambda target, p=p: held2[p].at[:, target]))
    flying, next_flying = next_flying, []
    for p in range(3):
        begin, width, order = PORTIONS[p]
        for copy in flying[p]:
            copy.wait_recv()
        left = [name for name in DIMS if name != order[0]]
        value = held2[p][me[order[1]]] if order[1] == left[0] else held2[p][:, me[order[1]]]
        value = value.astype(F32)
        for k in range(3):
            value = value + in2[p][k].astype(F32)
        held3[p][...] = value.astype(BF16)
        next_flying.append(start(p, 2, lambda target, p=p: held3[p].at[target]))
    for p in range(3):
        begin, width, order = PORTIONS[p]
        for copy in next_flying[p]:
            copy.wait_recv()
        value = held3[p][me[order[2]]].astype(F32)
        for k in range(3):
            value = value + in3[p][k].astype(F32)
        value = value + x_ref[:, begin : begin + width]
        if routed:
            own[:, begin : begin + width] = value.astype(BF16)
        else:
            out_ref[:, begin : begin + width] = value

    if routed:
        final_copies = []
        for i, to in enumerate(final_to):
            copy = remote(own, final_in.at[z, yh], final_s.at[i], final_r.at[i], to)
            copy.start()
            final_copies.append(copy)
        final_in[z, yh] = own[...]
        for copy in final_copies:
            copy.wait_recv()
        row = lax.broadcasted_iota(jnp.int32, (16, BLK), 0)
        for f in range(8):
            block = final_in[f // 2, f % 2].astype(F32)
            for t in range(2):
                out_ref[t : t + 1, f * BLK : (f + 1) * BLK] = jnp.sum(
                    jnp.where(row == f_me * 2 + t, block, 0.0), axis=0, keepdims=True
                )
        for copy in final_copies:
            copy.wait_send()
    for copy in sends + core_copies:
        copy.wait_send()


def ffn(routed, shard, gain, w_gate, w_up, w_down, w_router=None, ids=None):
    any_space = pl.BlockSpec(memory_space=pl.ANY)
    vmem = pl.BlockSpec(memory_space=pltpu.VMEM)
    dma = pltpu.SemaphoreType.DMA
    hidden = w_down.shape[0]
    widths = [width for _, width, _ in PORTIONS]
    extra_in, extra_specs, extra_scratch = [], [], []
    if routed:
        extra_in, extra_specs = [w_router, ids], [vmem, vmem]
        extra_scratch = [pltpu.VMEM((16, BLK), BF16), pltpu.VMEM((4, 2, 16, BLK), BF16), dma((7,)), dma((7,))]
    return pl.pallas_call(
        functools.partial(ffn_kernel, routed),
        out_shape=jax.ShapeDtypeStruct((2, D) if routed else (16, BLK), F32),
        in_specs=[vmem, vmem] + extra_specs + [any_space] * 3,
        out_specs=vmem,
        scratch_shapes=extra_scratch
        + [
            pltpu.VMEM(w_gate.shape, BF16),
            pltpu.VMEM(w_up.shape, BF16),
            pltpu.VMEM(w_down.shape, BF16),
            pltpu.VMEM((4, 4, 4, 2, 16, BLK), BF16),
            pltpu.VMEM((4, 4, 4, 2, 16, BLK), BF16),
            pltpu.VMEM((4, 4, 4, 16, BLK), BF16),
            pltpu.VMEM((2, 256, hidden), F32),
            pltpu.VMEM((256, 128), F32),
            pltpu.VMEM((256, 16), F32),
        ]
        + [pltpu.VMEM((3, 4, 4, 16, width), BF16) for width in widths]
        + [pltpu.VMEM((4, 4, 16, width), BF16) for width in widths]
        + [pltpu.VMEM((3, 4, 16, width), BF16) for width in widths]
        + [pltpu.VMEM((4, 16, width), BF16) for width in widths]
        + [pltpu.VMEM((3, 16, width), BF16) for width in widths]
        + [
            dma((3,)),
            dma((3, 3, 3)), dma((3, 3, 3)), dma((3, 4)), dma((3, 4)),
            dma((4,)), dma((4,)), dma((3, 3, 3)), dma((3, 3, 3)),
        ],
        compiler_params=pltpu.CompilerParams(
            collective_id=2 if routed else 1, has_side_effects=True, vmem_limit_bytes=VMEM_LIMIT
        ),
        name="routed_ffn" if routed else "dense_ffn",
    )(shard, gain, *extra_in, w_gate, w_up, w_down)


def latent_attention(queries, cache, new_latent, lengths, latent_dim):
    score_scale = (VD + ROPE) ** (-0.5)
    scores = (
        jnp.einsum("thc,tlc->thl", queries, cache, preferred_element_type=jnp.float32) * score_scale
    )
    own_score = (
        jnp.einsum("thc,tc->th", queries, new_latent, preferred_element_type=jnp.float32)
        * score_scale
    )
    places = jnp.arange(cache.shape[1], dtype=jnp.int32)
    in_range = places[None, None, :] < lengths[:, None, None]
    scores = jnp.where(in_range, scores, -jnp.inf)
    peak = jnp.maximum(jnp.max(scores, axis=2), own_score)
    weights = jnp.exp(scores - peak[:, :, None])
    own_weight = jnp.exp(own_score - peak)
    sum_total = jnp.sum(weights, axis=2) + own_weight
    probability = (weights / sum_total[:, :, None]).astype(jnp.bfloat16)
    own_probability = (own_weight / sum_total).astype(jnp.bfloat16)
    context = jnp.einsum(
        "thl,tlc->thc", probability, cache[:, :, :latent_dim], preferred_element_type=jnp.float32
    )
    context = context + own_probability.astype(jnp.float32)[:, :, None] * new_latent[
        :, None, :latent_dim
    ].astype(jnp.float32)
    return context.astype(jnp.bfloat16)


def body(
    hidden,
    queries,
    cache,
    new_latent,
    lengths,
    w_values,
    w_out,
    gain_attn,
    w_dense_gate,
    w_dense_up,
    w_dense_down,
    gain_moe,
    w_router,
    expert_ids,
    w_expert_gate,
    w_expert_up,
    w_expert_down,
):
    top_count = expert_ids.shape[1]
    everyone_ids = lax.all_gather(expert_ids, ("tp", "ep"), axis=0, tiled=True)
    ids = everyone_ids.reshape(8, 8, 2, 2, top_count).transpose(2, 0, 1, 3, 4).reshape(256, top_count)
    context = latent_attention(queries, cache, new_latent, lengths, w_values.shape[1])
    after_attn = attn_exchange(
        context.reshape(2, 8, 16, 512), hidden, w_values, jnp.swapaxes(w_out, 1, 2)
    )
    second = ffn(False, after_attn, gain_attn.reshape(8, BLK), w_dense_gate.T, w_dense_up.T, w_dense_down)
    out = ffn(
        True, second, gain_moe.reshape(8, BLK), w_expert_gate[0], w_expert_up[0], w_expert_down[0], w_router.T, ids
    )
    return out.astype(BF16)


def solution(mesh):
    in_specs = (
        P(("tp", "ep"), None),
        P(("tp", "ep"), None, None),
        P(("tp", "ep"), None, None),
        P(("tp", "ep"), None),
        P(("tp", "ep")),
        P("tp", None, None),
        P("tp", None, "ep"),
        P(),
        P(None, ("tp", "ep")),
        P(None, ("tp", "ep")),
        P(("tp", "ep"), None),
        P(),
        P(),
        P(("tp", "ep"), None),
        P("ep", None, "tp"),
        P("ep", None, "tp"),
        P("ep", "tp", None),
    )
    out_specs = P(("tp", "ep"), None)
    return jax.shard_map(body, mesh=mesh, in_specs=in_specs, out_specs=out_specs, check_vma=False)
```

time: 492 us -> 207 us (0.42)
  waiting for transfers between devices: 359 us -> 0 us
  Pallas kernels: 0 us -> 148 us
  matrix products: 37.4 us -> 4.28 us
  local copies, waits for them, and re-layouts: 23.8 us -> 2.14 us
  between operations: 13.7 us -> 0.08 us
  blocking collectives: 41.8 us -> 50 us
  starting transfers between devices: 7.37 us -> 0 us
  other arithmetic: 7.97 us -> 2.57 us
    unnamed x7 -> x0, waiting for transfers between devices: 156 us -> none
    pallas_call x0 -> x3, Pallas kernels: none -> 148 us  [the longest x2 114 us: ffn(): pl.pallas_call(functools.partial(ffn_kernel, routed), out_shape=jax.Shape...]
    all_gather x3 -> x0, waiting for transfers between devices: 128 us -> none  [the longest x1 61.6 us: body(): everyone = lax.all_gather(normed, ('tp', 'ep'), axis=0, tiled=True)]
    reduce_scatter x2 -> x0, waiting for transfers between devices: 65.3 us -> none  [the longest x1 35.5 us: body(): lax.psum_scatter(partial_out.astype(jnp.bfloat16), 'tp', scatter_dimensio...]
    all_gather x0 -> x1, blocking collectives: none -> 50 us  [body(): everyone_ids = lax.all_gather(expert_ids, ('tp', 'ep'), axis=0, tiled=True)]
    all_to_all x3 -> x0, blocking collectives: 41.8 us -> none  [the longest x1 15.7 us: body(): lax.all_to_all(outgoing, 'ep', split_axis=0, concat_axis=1, tiled=True)]
    dot_general x11 -> x0, matrix products: 32.9 us -> none  [the longest x1 10.5 us: body(): jnp.dot(dense_act, w_dense_down, preferred_element_type=jnp.float32)]
    unnamed x23 -> x12, local copies, waits for them, and re-layouts: 14.3 us -> 0.22 us
  transfers between devices with their start and end apart: 7 -> 0, of which waited for: 7 -> 0; matrix products, arithmetic and copies ran while one was open for 1% -> 0% of each run, Pallas kernels for 0% -> 0%
where the time goes in v1:
time: 207 us
  Pallas kernels  148 us (71%)
  blocking collectives  50 us (24%)
  matrix products  4.28 us (2%)
  other arithmetic  2.57 us (1%)
  local copies, waits for them, and re-layouts  2.14 us (1%)
    pallas_call x2, Pallas kernels, ffn(): pl.pallas_call(functools.partial(ffn_kernel, routed), out_shape=jax.Shape...  114 us
    all_gather x1, blocking collectives, body(): everyone_ids = lax.all_gather(expert_ids, ('tp', 'ep'), axis=0, tiled=True)  50 us
    pallas_call x1, Pallas kernels, attn_exchange(): pl.pallas_call(attn_kernel, out_shape=jax.ShapeDtypeStruct((16, BLK), F32...  33.9 us

profile of v1, /device:TPU:0, one launch (start us, length us, event | category | flops | bytes accessed | tf_op | source)
XLA Modules:
  0.0 206.7 jit_solution(12917814890993602473)
XLA Ops:
  0.0 0.0 copy-start
  0.0 0.0 copy-start.4
  0.0 0.8 iota_compare_fusion
  0.8 0.2 copy-done
  1.0 0.0 copy-start.1
  1.0 2.6 %fusion.16 = (f32[2,128]{1,0:T(2,128)S(1)}, f32[2,128,1024]{2,1,0:T(8,128)S(1)}) fusion(bf16[2,128,576]{1,2,0:T(8,128)(2,1)S(1)} %copy-done, bf16[2,1024,576]{1,2,0:T(8,128)(2,1)} %param.19, pred[2,1024]{1,0:T(4,128)(4,1)S(1)} %iota_compare_fusion), kind=kOutput, calls=%fused_computation.20 | convolution fusion | flops 302776064 | bytes 3705856 | tf_op jit(solution)/shard_map/thc,tlc->thl/dot_general | solution.py:482
  3.6 0.0 copy-done.4
  3.6 0.2 fusion.12
  3.7 0.3 fusion.9
  4.1 0.0 copy-done.1
  4.1 1.5 fusion.6
  5.6 0.0 copy-start.2
  5.6 33.9 %attn_exchange.1.refs_0_ = f32[16,896]{1,0:T(8,128)} custom-call(bf16[2,8,16,512]{3,2,1,0:T(8,128)(2,1)} %bitcast.27, bf16[2,7168]{1,0:T(2,128)(2,1)} %hid_ref.1, bf16[16,512,128]{2,1,0:T(8,128)(2,1)} %wv_hbm.1, bf16[16,448,128]{2,1,0:T(8,128)(2,1)} %bitcast.24), custom_call_target="tpu_custom_call" | custom-call | tf_op jit(solution)/shard_map/attn_exchange/pallas_call | solution.py:176
  39.5 0.0 copy-done.2
  39.5 0.6 reshape.42.refs_1_
  40.2 0.0 copy-start.5
  40.2 53.4 %dense_ffn.1.refs_0_ = f32[16,896]{1,0:T(8,128)} custom-call(f32[16,896]{1,0:T(8,128)} %attn_exchange.1.refs_0_, f32[8,896]{1,0:T(8,128)} %reshape.42.refs_1_, bf16[144,7168]{1,0:T(8,128)(2,1)} %bitcast.22, bf16[144,7168]{1,0:T(8,128)(2,1)} %bitcast.23, bf16[144,7168]{1,0:T(8,128)(2,1)} %refs_4_.1), custom_call_target="tpu_custom_call" | custom-call | tf_op jit(solution)/shard_map/dense_ffn/pallas_call | solution.py:445
  93.6 0.0 copy-done.5
  93.6 50.0 %all-gather = s32[128,2,8]{2,1,0:T(2,128)S(1)} all-gather(s32[1,2,8]{2,1,0:T(2,128)S(1)} %bitcast.32), channel_id=1, replica_groups=mesh['tp'=8,'ep'=16] {'tp','ep'}, dimensions={0}, use_global_device_ids=true | all-gather | bytes 8256 | tf_op jit(solution)/shard_map/all_gather | solution.py:526
  143.6 0.7 copy.21
  144.3 0.0 copy-done.3
  144.3 0.6 reshape.43.refs_1_
  144.9 60.3 %routed_ffn.1 = f32[2,7168]{1,0:T(2,128)} custom-call(f32[16,896]{1,0:T(8,128)} %dense_ffn.1.refs_0_, f32[8,896]{1,0:T(8,128)} %reshape.43.refs_1_, bf16[16,7168]{1,0:T(8,128)(2,1)} %bitcast.28, s32[256,8]{1,0:T(8,128)} %bitcast.25, bf16[7168,256]{1,0:T(8,128)(2,1)} %bitcast.19, bf16[7168,256]{1,0:T(8,128)(2,1)} %bitcast.20, bf16[256,7168]{1,0:T(8,128)(2,1)} %bitcast.21), custom_call_target="tpu_custom_call" | custom-call | tf_op jit(solution)/shard_map/routed_ffn/pallas_call | solution.py:445
  205.2 1.4 convert_element_type.24
  (4 shorter events, 0.0 us)
Async XLA Ops:
  0.0 1.0 copy-start
  0.0 3.6 %copy-start.4 = (bf16[2,576]{1,0:T(2,128)(2,1)S(1)}, bf16[2,576]{1,0:T(2,128)(2,1)}, u32[]{:S(2)}) copy-start(bf16[2,576]{1,0:T(2,128)(2,1)} %param.20) | copy-start | bytes 6916
  1.0 3.1 %copy-start.1 = (bf16[2,1024,576]{1,2,0:T(8,128)(2,1)S(1)}, bf16[2,1024,576]{1,2,0:T(8,128)(2,1)}, u32[]{:S(2)}) copy-start(bf16[2,1024,576]{1,2,0:T(8,128)(2,1)} %param.19) | copy-start | bytes 7077892
  5.6 33.9 %copy-start.2 = (f32[7168]{0:T(1024)S(1)}, f32[7168]{0:T(1024)}, u32[]{:S(2)}) copy-start(f32[7168]{0:T(1024)} %param.24) | copy-start | bytes 86020
  40.2 53.4 %copy-start.5 = (s32[2,8]{1,0:T(2,128)S(1)}, s32[2,8]{1,0:T(2,128)}, u32[]{:S(2)}) copy-start(s32[2,8]{1,0:T(2,128)} %param.30) | copy-start | bytes 196
  40.2 104.1 %copy-start.3 = (f32[7168]{0:T(1024)S(1)}, f32[7168]{0:T(1024)}, u32[]{:S(2)}) copy-start(f32[7168]{0:T(1024)} %param.28) | copy-start | bytes 86020

commit v2 on v1

v2 whole, which is shorter than its diff:
```python
import jax
import jax.numpy as jnp
from jax import lax
from jax.experimental import pallas as pl
from jax.experimental.pallas import tpu as pltpu
from jax.sharding import PartitionSpec as P

ROPE = 64
VD = 128
D = 7168
BLK = 896
EPSILON = 1e-06
ROUTE_SCALE = 2.5
MESH = pl.DeviceIdType.MESH
F32 = jnp.float32
BF16 = jnp.bfloat16
VMEM_LIMIT = 60 * 2**20


PORTIONS = ((0, 384, ("x", "y", "z")), (384, 256, ("y", "z", "x")), (640, 256, ("z", "x", "y")))
DIMS = ("z", "y", "x")


def coords():
    tp, ep = lax.axis_index("tp"), lax.axis_index("ep")
    return dict(x=tp // 2, c=tp % 2, z=ep // 4, y=ep % 4)


def device(at):
    return (at["x"] * 2 + at["c"], at["z"] * 4 + at["y"])


def moved(at, **steps):
    new = dict(at)
    for name, step in steps.items():
        new[name] = lax.rem(at[name] + step, 2 if name == "c" else 4)
    return new


def meet(partners):
    barrier = pltpu.get_barrier_semaphore()
    for partner in partners:
        pl.semaphore_signal(barrier, inc=1, device_id=device(partner), device_id_type=MESH)
    pl.semaphore_wait(barrier, len(partners))


def remote(src, dst, send, recv, partner):
    return pltpu.make_async_remote_copy(
        src_ref=src, dst_ref=dst, send_sem=send, recv_sem=recv, device_id=device(partner), device_id_type=MESH
    )


def dot_nt(a, b):
    return lax.dot_general(a, b, (((1,), (1,)), ((), ())), preferred_element_type=F32)


def dot(a, b):
    return jnp.dot(a, b, preferred_element_type=F32)


def attn_kernel(
    ctx_ref, hid_ref, ids_ref, wv_hbm, wo_hbm, out_ref, chosen_ref,
    wv, wo, ctx_in, heads, part, part_in, hid_out, hid_in, mask_out, mask_in, load_sem,
    hid_s, hid_r, ctx_s, ctx_r, mask_s, mask_r, hv_s, hv_r, part_s, part_r,
):
    me = coords()
    x, c, z, y = me["x"], me["c"], me["z"], me["y"]
    yh, yl = y // 2, y % 2
    tp = x * 2 + c
    pad = pl.multiple_of(yl * 64, 64)
    load_wv = pltpu.make_async_copy(wv_hbm, wv, load_sem.at[0])
    load_wo = pltpu.make_async_copy(wo_hbm, wo.at[:, pl.ds(pad, 448), :], load_sem.at[1])
    load_wv.start()
    load_wo.start()
    wo[:, pl.ds(pl.multiple_of((1 - yl) * 448, 64), 64), :] = jnp.zeros((16, 64, 128), BF16)

    def at_tp(step):
        other = lax.rem(tp + step, 8)
        return dict(me, x=other // 2, c=other % 2)

    tp_steps = [(dt, dy) for dy in (0, 1) for dt in range(8) if dt or dy]
    part_to = [dict(at_tp(dt), y=yh * 2 + (yl + dy) % 2) for dt, dy in tp_steps]
    hid_steps = [(dz, dy) for dy in (0, 2) for dz in range(4) if dz or dy]
    hid_to = [moved(me, z=dz, y=dy) for dz, dy in hid_steps]
    other_odd = dict(me, y=lax.rem(yh * 2 + 2, 4) + (1 - yl))
    meet(part_to + hid_to + [other_odd])

    first = (z * 2 + yh) * 2
    row = lax.broadcasted_iota(jnp.int32, (16, BLK), 0)
    for f in range(8):
        both = hid_ref[:, f * BLK : (f + 1) * BLK].astype(F32)
        placed = jnp.where(row == first, both[0:1, :], jnp.where(row == first + 1, both[1:2, :], 0.0))
        hid_out[f // 2, f % 2] = placed.astype(BF16)
    lane = lax.broadcasted_iota(jnp.int32, (2, 128), 1)
    chosen = jnp.zeros((2, 128), F32)
    for k in range(ids_ref.shape[1]):
        chosen = chosen + jnp.where(ids_ref[:, k : k + 1] == lane, 1.0, 0.0)
    row = lax.broadcasted_iota(jnp.int32, (16, 128), 0)
    placed = jnp.where(row == tp * 2, chosen[0:1, :], jnp.where(row == tp * 2 + 1, chosen[1:2, :], 0.0))
    mask_out[...] = placed.astype(BF16)
    ctx_copies = []
    for step in range(1, 8):
        to = at_tp(step)
        copy = remote(ctx_ref.at[:, to["x"] * 2 + to["c"]], ctx_in.at[tp], ctx_s.at[step - 1], ctx_r.at[step - 1], to)
        copy.start()
        ctx_copies.append(copy)
    for step in range(1, 8):
        copy = remote(mask_out, mask_in.at[tp], mask_s.at[step - 1], mask_r.at[step - 1], at_tp(step))
        copy.start()
        ctx_copies.append(copy)
    hid_copies = []
    for i, to in enumerate(hid_to):
        copy = remote(hid_out.at[to["z"], to["y"] // 2], hid_in.at[z, yh], hid_s.at[i], hid_r.at[i], to)
        copy.start()
        hid_copies.append(copy)
    ctx_in[tp] = ctx_ref[:, tp]
    mask_in[tp] = mask_out[...]
    hid_in[z, yh] = hid_out[z, yh]
    for copy in ctx_copies:
        copy.wait_recv()
    load_wv.wait()

    i = lax.broadcasted_iota(jnp.int32, (256, 256), 0)
    j = lax.broadcasted_iota(jnp.int32, (256, 256), 1)
    turn = ((i & 15) * 16 + (i >> 4) == j).astype(BF16)
    by_head = dot(turn, ctx_in[...].reshape(256, 512)).astype(BF16)
    for h in range(16):
        heads[z, y, :, h * 128 : (h + 1) * 128] = dot(by_head[h * 16 : (h + 1) * 16, :], wv[h]).astype(BF16)

    heads[z, y, :, 2048:2176] = jnp.sum(mask_in[...].astype(F32), axis=0).astype(BF16)

    halves = ((0, "z", "y"), (1, "y", "z"))
    sends = []
    for half, one, two in halves:
        lanes = pl.ds(half * 1024, 1024 + half * 128)
        for step in range(1, 4):
            mine = heads.at[z, y, :, lanes]
            copy = remote(mine, mine, hv_s.at[half, 0, step - 1], hv_r.at[half, 0, step - 1], moved(me, **{one: step}))
            copy.start()
            sends.append(copy)
    for half, one, two in halves:
        lanes = pl.ds(half * 1024, 1024 + half * 128)
        for step in range(1, 4):
            sends[half * 3 + step - 1].wait_recv()
        for step in range(1, 4):
            slab = heads.at[:, y, :, lanes] if two == "y" else heads.at[z, :, :, lanes]
            copy = remote(slab, slab, hv_s.at[half, 1, step - 1], hv_r.at[half, 1, step - 1], moved(me, **{two: step}))
            copy.start()
            sends.append(copy)
    load_wo.wait()
    for copy in sends[6:]:
        copy.wait_recv()

    total = jnp.zeros((256, 512), F32)
    for pair in range(8):
        rows = heads[:, :, :, pair * 256 : (pair + 1) * 256].reshape(256, 256)
        weights = jnp.concatenate([wo[2 * pair], wo[2 * pair + 1]], axis=1)
        total = total + dot_nt(rows, weights)
    t, from_yh, from_z = i & 1, (i >> 1) & 1, (i >> 2) & 3
    source = from_z * 64 + (from_yh * 2 + (i >> 7)) * 16 + ((i >> 4) & 7) * 2 + t
    order = (source == j).astype(BF16)
    part[...] = dot(order, total.astype(BF16)).astype(BF16).reshape(2, 8, 16, 512)
    part_copies = []
    for i_to, to in enumerate(part_to):
        copy = remote(
            part.at[to["y"] % 2, to["x"] * 2 + to["c"]], part_in.at[yl, tp], part_s.at[i_to], part_r.at[i_to], to
        )
        copy.start()
        part_copies.append(copy)
    part_in[yl, tp] = part[yl, tp]
    plane = i >> 7
    to_yl = ((i >> 6) & 1) * (1 - plane) + ((i >> 4) & 1) * plane
    to_x = ((i >> 4) & 3) * (1 - plane) + ((i >> 5) & 3) * plane
    source = from_z * 64 + (from_yh * 2 + to_yl) * 16 + to_x * 4 + plane * 2 + t
    chosen_ref[...] = dot((source == j).astype(BF16), heads[:, :, :, 2048:2176].reshape(256, 128)).astype(BF16)
    for copy in hid_copies:
        copy.wait_recv()
    out_ref[...] = jnp.sum(hid_in[...].astype(F32), axis=(0, 1))
    for copy in part_copies:
        copy.wait_recv()
    sums = jnp.sum(part_in[...].astype(F32), axis=1)
    out_ref[:, 0:512] += sums[0]
    out_ref[:, 384:896] += sums[1]
    for copy in ctx_copies + hid_copies + sends + part_copies:
        copy.wait_send()


def attn_exchange(context, hidden, ids, w_values, w_out):
    any_space = pl.BlockSpec(memory_space=pl.ANY)
    vmem = pl.BlockSpec(memory_space=pltpu.VMEM)
    dma = pltpu.SemaphoreType.DMA
    return pl.pallas_call(
        attn_kernel,
        out_shape=(jax.ShapeDtypeStruct((16, BLK), F32), jax.ShapeDtypeStruct((256, 128), BF16)),
        in_specs=[vmem, vmem, vmem, any_space, any_space],
        out_specs=(vmem, vmem),
        scratch_shapes=[
            pltpu.VMEM((16, 512, 128), BF16),
            pltpu.VMEM((16, 512, 128), BF16),
            pltpu.VMEM((8, 2, 16, 512), BF16),
            pltpu.VMEM((4, 4, 16, 2176), BF16),
            pltpu.VMEM((2, 8, 16, 512), BF16),
            pltpu.VMEM((2, 8, 16, 512), BF16),
            pltpu.VMEM((4, 2, 16, BLK), BF16),
            pltpu.VMEM((4, 2, 16, BLK), BF16),
            pltpu.VMEM((16, 128), BF16),
            pltpu.VMEM((8, 16, 128), BF16),
            dma((2,)),
            dma((7,)), dma((7,)), dma((7,)), dma((7,)), dma((7,)), dma((7,)),
            dma((2, 2, 3)), dma((2, 2, 3)), dma((15,)), dma((15,)),
        ],
        compiler_params=pltpu.CompilerParams(collective_id=0, has_side_effects=True, vmem_limit_bytes=VMEM_LIMIT),
        name="attn_exchange",
    )(context, hidden, ids, w_values, w_out)


def turned(at):
    c = at["c"]
    return dict(
        z=at["z"] * (1 - c) + at["x"] * c, y=at["y"] * (1 - c) + at["z"] * c, x=at["x"] * (1 - c) + at["y"] * c, c=c
    )


def straight(at):
    c = at["c"]
    return dict(
        z=at["z"] * (1 - c) + at["y"] * c, y=at["y"] * (1 - c) + at["x"] * c, x=at["x"] * (1 - c) + at["z"] * c, c=c
    )


def region_of(at, portion, phase):
    start, width, order = PORTIONS[portion]
    done = order[::-1][:phase]
    index = tuple(pl.ds(0, 4) if name in done else at[name] for name in DIMS)
    return (at["c"],) + index + (slice(None), pl.ds(start, width))


def plane_cut(plane, part, half=None):
    ys = slice(None) if half is None else slice(half * 2, half * 2 + 2)
    return (0, part, ys) if plane == 0 else (1, slice(None), part, ys)


class Layer:
    def __init__(self, number, me, sibling, x_ref, gain_ref, refs):
        self.number, self.me, self.sibling, self.x, self.gain = number, me, sibling, x_ref, gain_ref
        (
            self.full, self.partial, self.core_in, self.acc, self.square,
            *lists, self.gather_s, self.gather_r, self.pair_s, self.pair_r, self.core_s, self.core_r, self.sum_s, self.sum_r,
        ) = refs
        self.in1, self.held2, self.in2, self.held3, self.in3 = [lists[i * 3 : i * 3 + 3] for i in range(5)]
        self.ring = {name: [moved(me, **{name: step}) for step in (1, 2, 3)] for name in DIMS}
        self.back = {name: [moved(me, **{name: 4 - step}) for step in (1, 2, 3)] for name in DIMS}
        self.sends = []

    def begin(self, p, f_me):
        start, width, order = PORTIONS[p]
        me = self.me
        lanes = pl.ds(start, width)
        scaled = self.x[:, lanes] * self.gain[pl.ds(f_me, 1), lanes]
        self.full[me["c"], me["z"], me["y"], me["x"], :, lanes] = scaled.astype(BF16)
        self.send(p, 0)

    def send(self, p, phase):
        axis = PORTIONS[p][2][2 - phase]
        region = self.full.at[region_of(self.me, p, phase)]
        for k in range(3):
            copy = remote(
                region, region, self.gather_s.at[p, phase, k], self.gather_r.at[p, phase, k], straight(self.ring[axis][k])
            )
            copy.start()
            self.sends.append(copy)

    def take(self, p, phase, k):
        axis = PORTIONS[p][2][2 - phase]
        region = self.full.at[region_of(self.back[axis][k], p, phase)]
        remote(
            region, region, self.gather_s.at[p, phase, k], self.gather_r.at[p, phase, k], straight(self.ring[axis][k])
        ).wait_recv()
        return region

    def pair(self, p, k, plane):
        place = self.me if k == 3 else self.back[PORTIONS[p][2][0]][k]
        region = self.full.at[region_of(dict(place, c=plane), p, 2)]
        return remote(region, region, self.pair_s.at[p, k], self.pair_r.at[p, k], self.sibling)

    def spread(self):
        for phase in (1, 2):
            for p in range(3):
                for k in range(3):
                    self.take(p, phase - 1, k)
                self.send(p, phase)
                if phase == 2:
                    self.pair(p, 3, self.me["c"]).start()

    def forward(self):
        for k in (0, 2, 1):
            for p in range(3):
                self.take(p, 2, k)
                self.pair(p, k, self.me["c"]).start()

    def take_pair(self, plane):
        other = turned(self.sibling_real)
        for k in (3, 0, 2, 1):
            for p in range(3):
                axis = PORTIONS[p][2][0]
                place = other if k == 3 else moved(other, **{axis: 3 - k})
                region = self.full.at[region_of(dict(place, c=plane), p, 2)]
                remote(region, region, self.pair_s.at[p, k], self.pair_r.at[p, k], self.sibling).wait_recv()

    def core_copy(self, plane, part):
        cut = plane_cut(plane, part)
        return remote(
            self.partial.at[cut], self.core_in.at[cut[1:]], self.core_s.at[part], self.core_r.at[part], self.sibling
        )

    def core_sum(self, plane):
        for part in range(4):
            self.core_copy(plane, part).wait_recv()

            def add(row, carry, part=part):
                cut = (0, part, row) if plane == 0 else (1, row, part)
                both = self.partial[cut].astype(F32) + self.core_in[cut[1:]].astype(F32)
                self.partial[cut] = both.astype(BF16)
                return carry

            lax.fori_loop(0, 4, add, 0)

    def start(self, p, phase, source):
        axis = PORTIONS[p][2][phase]
        into = (self.in1, self.in2, self.in3)[phase][p]
        copies = []
        for k in range(3):
            to = self.ring[axis][k]
            copy = remote(
                source(to[axis]), into.at[k], self.sum_s.at[p, phase, k], self.sum_r.at[p, phase, k], straight(to)
            )
            copies.append(copy)
        return copies

    def first_sums(self, p):
        begin, width, order = PORTIONS[p]

        def source(target):
            index = [slice(None)] * 3
            index[DIMS.index(order[0])] = target
            return self.partial.at[(self.me["c"],) + tuple(index) + (slice(None), pl.ds(begin, width))]

        return self.start(p, 0, source)

    def sums(self, finish):
        me = self.me
        second, third = [], []
        for p in range(3):
            begin, width, order = PORTIONS[p]
            for copy in self.first_sums(p):
                copy.wait_recv()
            left = [name for name in DIMS if name != order[0]]

            def add(i, carry, p=p, begin=begin, width=width, order=order, left=left):
                index = {order[0]: me[order[0]], left[0]: i, left[1]: slice(None)}
                index = (me["c"],) + tuple(index[name] for name in DIMS) + (slice(None), pl.ds(begin, width))
                value = self.partial[index].astype(F32)
                for k in range(3):
                    value = value + self.in1[p][k, i].astype(F32)
                self.held2[p][i] = value.astype(BF16)
                return carry

            lax.fori_loop(0, 4, add, 0)
            if order[1] == left[0]:
                second.append(self.start(p, 1, lambda target, p=p: self.held2[p].at[target]))
            else:
                second.append(self.start(p, 1, lambda target, p=p: self.held2[p].at[:, target]))
            for copy in second[p]:
                copy.start()
        for p in range(3):
            begin, width, order = PORTIONS[p]
            for copy in second[p]:
                copy.wait_recv()
            left = [name for name in DIMS if name != order[0]]
            mine = me[order[1]]
            value = self.held2[p][mine] if order[1] == left[0] else self.held2[p][:, mine]
            value = value.astype(F32)
            for k in range(3):
                value = value + self.in2[p][k].astype(F32)
            self.held3[p][...] = value.astype(BF16)
            third.append(self.start(p, 2, lambda target, p=p: self.held3[p].at[target]))
            for copy in third[p]:
                copy.start()
        for p in range(3):
            begin, width, order = PORTIONS[p]
            for copy in third[p]:
                copy.wait_recv()
            value = self.held3[p][me[order[2]]].astype(F32)
            for k in range(3):
                value = value + self.in3[p][k].astype(F32)
            finish(p, begin, width, value + self.x[:, begin : begin + width])
        self.sends += second[0] + second[1] + second[2] + third[0] + third[1] + third[2]

    def run(self, multiply, activate, down):
        c = self.me["c"]
        self.spread()
        for plane in (0, 1):

            @pl.when(c == plane)
            def _():
                self.forward()

            @pl.when(c != plane)
            def _(plane=plane):
                self.take_pair(plane)

            self.acc[...] = jnp.zeros_like(self.acc)
            self.square[...] = jnp.zeros_like(self.square)

            def step(f, carry, plane=plane):
                part, ys = f // 2, pl.ds((f % 2) * 2, 2)
                rows = self.full[0, part, ys] if plane == 0 else self.full[1, :, part, ys]
                rows = rows.reshape(128, BLK)
                multiply(rows, pl.ds(pl.multiple_of(f * BLK, 128), BLK))
                plain = rows.astype(F32) * (1.0 / self.gain[pl.ds(f, 1), :])
                plain = plain * plain
                piece = plain[:, 0:128]
                for k in range(1, 7):
                    piece = piece + plain[:, k * 128 : (k + 1) * 128]
                self.square[...] += piece
                return carry

            lax.fori_loop(0, 8, step, 0)
            scale = lax.rsqrt(jnp.sum(self.square[...], axis=1, keepdims=True) * (1.0 / D) + EPSILON)
            act = activate(plane, scale)
            for part in range(4):
                for half in range(2):
                    block = down(act, part * 2 + half).astype(BF16)
                    shape = (2, 4, 16, BLK) if plane == 0 else (4, 2, 16, BLK)
                    self.partial[plane_cut(plane, part, half)] = block.reshape(shape)

                @pl.when(c != plane)
                def _(plane=plane, part=part):
                    self.core_copy(plane, part).start()

            @pl.when(c == plane)
            def _(plane=plane):
                self.core_sum(plane)
                for p in range(3):
                    for copy in self.first_sums(p):
                        copy.start()

    def end(self):
        c = self.me["c"]
        for copy in self.sends:
            copy.wait_send()
        for p in range(3):
            for k in range(4):
                self.pair(p, k, c).wait_send()
            for copy in self.first_sums(p):
                copy.wait_send()
        for plane in (0, 1):

            @pl.when(c != plane)
            def _(plane=plane):
                for part in range(4):
                    self.core_copy(plane, part).wait_send()


def silu(value):
    return value / (1.0 + jnp.exp(-value))


def ffn_kernel(
    x_ref, gain1_ref, gain2_ref, wr_ref, chosen_ref, wg1_hbm, wu1_hbm, wd1_hbm, wg2_hbm, wu2_hbm, wd2_hbm, out_ref,
    wg1, wu1, wd1, wg2, wu2, wd2, mid, router_acc, own, final_in, load_sem, final_s, final_r, *refs,
):
    here = coords()
    f_me = here["z"] * 2 + here["y"] // 2
    yh = here["y"] // 2
    me = turned(here)
    sibling = moved(here, c=1)
    pairs = ((wg1_hbm, wg1), (wu1_hbm, wu1), (wd1_hbm, wd1), (wg2_hbm, wg2), (wu2_hbm, wu2), (wd2_hbm, wd2))
    loads = [pltpu.make_async_copy(src, dst, load_sem.at[i]) for i, (src, dst) in enumerate(pairs)]
    for load in loads:
        load.start()
    half = len(refs) // 2
    dense = Layer(0, me, sibling, x_ref, gain1_ref, refs[:half])
    routed = Layer(1, me, sibling, mid, gain2_ref, refs[half:])
    dense.sibling_real = routed.sibling_real = sibling
    final_steps = [(dz, dy) for dy in (0, 2) for dz in range(4) if dz or dy]
    final_to = [moved(here, z=dz, y=dy) for dz, dy in final_steps]
    partners = [moved(here, **{name: step}) for name in DIMS for step in (1, 2, 3)] + [sibling]
    meet(partners + [moved(here, z=dz, y=2) for dz in (1, 2, 3)])

    for p in range(3):
        dense.begin(p, f_me)
    for load in loads[:3]:
        load.wait()

    def multiply_dense(rows, at):
        dense.acc[0] += dot_nt(rows, wg1[:, at])
        dense.acc[1] += dot_nt(rows, wu1[:, at])

    def activate_dense(plane, scale):
        return (silu(dense.acc[0] * scale) * (dense.acc[1] * scale)).astype(BF16)

    def down_dense(act, f):
        return dot(act, wd1[:, f * BLK : (f + 1) * BLK])

    dense.run(multiply_dense, activate_dense, down_dense)

    def between(p, begin, width, value):
        mid[:, begin : begin + width] = value
        routed.begin(p, f_me)

    dense.sums(between)
    for load in loads[3:]:
        load.wait()

    def multiply_routed(rows, at):
        routed.acc[0] += dot(rows, wg2[at, :])
        routed.acc[1] += dot(rows, wu2[at, :])
        router_acc[...] += dot_nt(rows, wr_ref[:, at])

    def activate_routed(plane, scale):
        affinity = 1.0 / (1.0 + jnp.exp(-(router_acc[...] * scale)))
        router_acc[...] = jnp.zeros_like(router_acc)
        chosen = chosen_ref[plane * 128 : plane * 128 + 128, 0:16].astype(F32)
        picked = jnp.where(chosen > 0.5, affinity, 0.0)
        below = jnp.sum(picked, axis=1, keepdims=True)
        mine = lax.broadcasted_iota(jnp.int32, (128, 16), 1) == here["z"] * 4 + here["y"]
        weight = ROUTE_SCALE * jnp.sum(jnp.where(mine, picked, 0.0), axis=1, keepdims=True) / below
        wanted = jnp.sum(jnp.where(mine, chosen, 0.0), axis=1, keepdims=True) > 0.5
        act = silu(routed.acc[0] * scale) * (routed.acc[1] * scale)
        return jnp.where(wanted, act * weight, 0.0).astype(BF16)

    def down_routed(act, f):
        return dot(act, wd2[:, f * BLK : (f + 1) * BLK])

    router_acc[...] = jnp.zeros_like(router_acc)
    routed.run(multiply_routed, activate_routed, down_routed)

    def last(p, begin, width, value):
        own[:, begin : begin + width] = value.astype(BF16)

    routed.sums(last)

    final_copies = []
    for i, to in enumerate(final_to):
        copy = remote(own, final_in.at[here["z"], yh], final_s.at[i], final_r.at[i], to)
        copy.start()
        final_copies.append(copy)
    final_in[here["z"], yh] = own[...]
    for copy in final_copies:
        copy.wait_recv()
    row = lax.broadcasted_iota(jnp.int32, (16, BLK), 0)
    for f in range(8):
        block = final_in[f // 2, f % 2].astype(F32)
        for t in range(2):
            out_ref[t : t + 1, f * BLK : (f + 1) * BLK] = jnp.sum(
                jnp.where(row == f_me * 2 + t, block, 0.0), axis=0, keepdims=True
            )
    for copy in final_copies:
        copy.wait_send()
    dense.end()
    routed.end()


def layer_scratch(hidden):
    dma = pltpu.SemaphoreType.DMA
    widths = [width for _, width, _ in PORTIONS]
    return (
        [
            pltpu.VMEM((2, 4, 4, 4, 16, BLK), BF16),
            pltpu.VMEM((2, 4, 4, 4, 16, BLK), BF16),
            pltpu.VMEM((4, 4, 4, 16, BLK), BF16),
            pltpu.VMEM((2, 128, hidden), F32),
            pltpu.VMEM((128, 128), F32),
        ]
        + [pltpu.VMEM((3, 4, 4, 16, width), BF16) for width in widths]
        + [pltpu.VMEM((4, 4, 16, width), BF16) for width in widths]
        + [pltpu.VMEM((3, 4, 16, width), BF16) for width in widths]
        + [pltpu.VMEM((4, 16, width), BF16) for width in widths]
        + [pltpu.VMEM((3, 16, width), BF16) for width in widths]
        + [
            dma((3, 3, 3)), dma((3, 3, 3)), dma((3, 4)), dma((3, 4)),
            dma((4,)), dma((4,)), dma((3, 3, 3)), dma((3, 3, 3)),
        ]
    )


def feed_forwards(shard, gain1, gain2, w_router, chosen, dense, expert):
    any_space = pl.BlockSpec(memory_space=pl.ANY)
    vmem = pl.BlockSpec(memory_space=pltpu.VMEM)
    dma = pltpu.SemaphoreType.DMA
    return pl.pallas_call(
        ffn_kernel,
        out_shape=jax.ShapeDtypeStruct((2, D), F32),
        in_specs=[vmem] * 5 + [any_space] * 6,
        out_specs=vmem,
        scratch_shapes=[pltpu.VMEM(w.shape, BF16) for w in dense + expert]
        + [
            pltpu.VMEM((16, BLK), F32),
            pltpu.VMEM((128, 16), F32),
            pltpu.VMEM((16, BLK), BF16),
            pltpu.VMEM((4, 2, 16, BLK), BF16),
            dma((6,)), dma((7,)), dma((7,)),
        ]
        + layer_scratch(dense[2].shape[0])
        + layer_scratch(expert[2].shape[0]),
        compiler_params=pltpu.CompilerParams(collective_id=1, has_side_effects=True, vmem_limit_bytes=VMEM_LIMIT),
        name="feed_forwards",
    )(shard, gain1, gain2, w_router, chosen, *dense, *expert)


def latent_attention(queries, cache, new_latent, lengths, latent_dim):
    score_scale = (VD + ROPE) ** (-0.5)
    scores = (
        jnp.einsum("thc,tlc->thl", queries, cache, preferred_element_type=jnp.float32) * score_scale
    )
    own_score = (
        jnp.einsum("thc,tc->th", queries, new_latent, preferred_element_type=jnp.float32)
        * score_scale
    )
    places = jnp.arange(cache.shape[1], dtype=jnp.int32)
    in_range = places[None, None, :] < lengths[:, None, None]
    scores = jnp.where(in_range, scores, -jnp.inf)
    peak = jnp.maximum(jnp.max(scores, axis=2), own_score)
    weights = jnp.exp(scores - peak[:, :, None])
    own_weight = jnp.exp(own_score - peak)
    sum_total = jnp.sum(weights, axis=2) + own_weight
    probability = (weights / sum_total[:, :, None]).astype(jnp.bfloat16)
    own_probability = (own_weight / sum_total).astype(jnp.bfloat16)
    context = jnp.einsum(
        "thl,tlc->thc", probability, cache[:, :, :latent_dim], preferred_element_type=jnp.float32
    )
    context = context + own_probability.astype(jnp.float32)[:, :, None] * new_latent[
        :, None, :latent_dim
    ].astype(jnp.float32)
    return context.astype(jnp.bfloat16)


def body(
    hidden,
    queries,
    cache,
    new_latent,
    lengths,
    w_values,
    w_out,
    gain_attn,
    w_dense_gate,
    w_dense_up,
    w_dense_down,
    gain_moe,
    w_router,
    expert_ids,
    w_expert_gate,
    w_expert_up,
    w_expert_down,
):
    context = latent_attention(queries, cache, new_latent, lengths, w_values.shape[1])
    after_attn, chosen = attn_exchange(
        context.reshape(2, 8, 16, 512), hidden, expert_ids, w_values, jnp.swapaxes(w_out, 1, 2)
    )
    out = feed_forwards(
        after_attn,
        gain_attn.reshape(8, BLK),
        gain_moe.reshape(8, BLK),
        w_router.T,
        chosen,
        (w_dense_gate.T, w_dense_up.T, w_dense_down),
        (w_expert_gate[0], w_expert_up[0], w_expert_down[0]),
    )
    return out.astype(BF16)


def solution(mesh):
    in_specs = (
        P(("tp", "ep"), None),
        P(("tp", "ep"), None, None),
        P(("tp", "ep"), None, None),
        P(("tp", "ep"), None),
        P(("tp", "ep")),
        P("tp", None, None),
        P("tp", None, "ep"),
        P(),
        P(None, ("tp", "ep")),
        P(None, ("tp", "ep")),
        P(("tp", "ep"), None),
        P(),
        P(),
        P(("tp", "ep"), None),
        P("ep", None, "tp"),
        P("ep", None, "tp"),
        P("ep", "tp", None),
    )
    out_specs = P(("tp", "ep"), None)
    return jax.shard_map(body, mesh=mesh, in_specs=in_specs, out_specs=out_specs, check_vma=False)
```

time: 207 us -> 148 us (0.71)
  the two profiles are of different devices: /device:TPU:0 before, /device:TPU:1 now
where the time goes in v2:
time: 148 us
  Pallas kernels  140 us (95%)
  matrix products  4.28 us (3%)
  other arithmetic  2.57 us (2%)
    pallas_call x1, Pallas kernels, feed_forwards(): pl.pallas_call(ffn_kernel, out_shape=jax.ShapeDtypeStruct((2, D), F32), i...  104 us
    pallas_call x1, Pallas kernels, attn_exchange(): pl.pallas_call(attn_kernel, out_shape=(jax.ShapeDtypeStruct((16, BLK), F3...  35.8 us

profile of v2, /device:TPU:1, one launch (start us, length us, event | category | flops | bytes accessed | tf_op | source)
XLA Modules:
  0.0 148.1 jit_solution(9925217883023020881)
XLA Ops:
  0.0 0.0 copy-start
  0.0 0.0 copy-start.4
  0.0 0.8 iota_compare_fusion
  0.8 0.2 copy-done
  1.0 0.0 copy-start.1
  1.0 2.6 %fusion.16 = (f32[2,128]{1,0:T(2,128)S(1)}, f32[2,128,1024]{2,1,0:T(8,128)S(1)}) fusion(bf16[2,128,576]{1,2,0:T(8,128)(2,1)S(1)} %copy-done, bf16[2,1024,576]{1,2,0:T(8,128)(2,1)} %param.19, pred[2,1024]{1,0:T(4,128)(4,1)S(1)} %iota_compare_fusion), kind=kOutput, calls=%fused_computation.20 | convolution fusion | flops 302776064 | bytes 3705856 | tf_op jit(solution)/shard_map/thc,tlc->thl/dot_general | solution.py:615
  3.6 0.0 copy-done.4
  3.6 0.2 fusion.12
  3.7 0.3 fusion.9
  4.1 0.0 copy-done.1
  4.1 1.5 %fusion.6 = bf16[2,128,512]{2,1,0:T(8,128)(2,1)} fusion(bf16[2,1024,576]{1,2,0:T(8,128)(2,1)S(1)} %copy-done.1, f32[2,128,1024]{2,1,0:T(8,128)S(1)} %get-tuple-element.12, f32[2,128]{1,0:T(2,128)S(1)} %get-tuple-element.10, f32[2,128]{1,0:T(2,128)S(1)} %multiply_maximum_fusion, f32[2,512]{1,0:T(2,128)S(1)} %slice_convert_fusion, ...), kind=kOutput, calls=%fused_computation.5 | convolution fusion | flops 269615104 | bytes 3415040 | tf_op jit(solution)/shard_map/thl,tlc->thc/dot_general | solution.py:630
  5.6 0.0 copy-start.2
  5.6 0.0 copy-start.3
  5.7 35.8 %attn_exchange.1 = (f32[16,896]{1,0:T(8,128)}, bf16[256,128]{1,0:T(8,128)(2,1)}) custom-call(bf16[2,8,16,512]{3,2,1,0:T(8,128)(2,1)} %bitcast.20, bf16[2,7168]{1,0:T(2,128)(2,1)} %hid_ref.1, s32[2,8]{1,0:T(2,128)} %ids_ref.1, bf16[16,512,128]{2,1,0:T(8,128)(2,1)} %wv_hbm.1, bf16[16,448,128]{2,1,0:T(8,128)(2,1)} %bitcast.19), custom_call_target="tpu_custom_call" | custom-call | tf_op jit(solution)/shard_map/attn_exchange/pallas_call | solution.py:192
  41.5 0.0 copy-done.2
  41.5 0.6 reshape.36.gain1_ref
  42.1 0.0 copy-done.3
  42.1 0.6 reshape.37.gain2_ref
  42.7 103.9 %feed_forwards.1 = f32[2,7168]{1,0:T(2,128)} custom-call(f32[16,896]{1,0:T(8,128)} %get-tuple-element.7.x_ref, f32[8,896]{1,0:T(8,128)} %reshape.36.gain1_ref, f32[8,896]{1,0:T(8,128)} %reshape.37.gain2_ref, bf16[16,7168]{1,0:T(8,128)(2,1)} %bitcast.21, bf16[256,128]{1,0:T(8,128)(2,1)} %get-tuple-element.8.chosen_ref, bf16[144,7168]{1,0:T(8,128)(2,1)} %bitcast.17, ...), custom_call_target="tpu_custom_call" | custom-call | tf_op jit(solution)/shard_map/feed_forwards/pallas_call | solution.py:592
  146.6 1.4 convert_element_type.24
  (3 shorter events, 0.0 us)
Async XLA Ops:
  0.0 1.0 copy-start
  0.0 3.6 %copy-start.4 = (bf16[2,576]{1,0:T(2,128)(2,1)S(1)}, bf16[2,576]{1,0:T(2,128)(2,1)}, u32[]{:S(2)}) copy-start(bf16[2,576]{1,0:T(2,128)(2,1)} %param.20) | copy-start | bytes 6916
  1.0 3.1 %copy-start.1 = (bf16[2,1024,576]{1,2,0:T(8,128)(2,1)S(1)}, bf16[2,1024,576]{1,2,0:T(8,128)(2,1)}, u32[]{:S(2)}) copy-start(bf16[2,1024,576]{1,2,0:T(8,128)(2,1)} %param.19) | copy-start | bytes 7077892
  5.6 35.8 %copy-start.2 = (f32[7168]{0:T(1024)S(1)}, f32[7168]{0:T(1024)}, u32[]{:S(2)}) copy-start(f32[7168]{0:T(1024)} %param.24) | copy-start | bytes 86020
  5.6 36.5 %copy-start.3 = (f32[7168]{0:T(1024)S(1)}, f32[7168]{0:T(1024)}, u32[]{:S(2)}) copy-start(f32[7168]{0:T(1024)} %param.28) | copy-start | bytes 86020

commit v3 on v2

--- a/solution.py
+++ b/solution.py
@@ -9,6 +9,7 @@
 VD = 128
 D = 7168
 BLK = 896
+UP_AT = 384
 EPSILON = 1e-06
 ROUTE_SCALE = 2.5
 MESH = pl.DeviceIdType.MESH
@@ -19,6 +20,7 @@
 
 PORTIONS = ((0, 384, ("x", "y", "z")), (384, 256, ("y", "z", "x")), (640, 256, ("z", "x", "y")))
 DIMS = ("z", "y", "x")
+PLANE = sorted(((i, j) for i in range(4) for j in range(4) if i or j), key=lambda d: -sum(min(k, 4 - k) for k in d))
 
 
 def coords():
@@ -232,22 +234,21 @@
     start, width, order = PORTIONS[portion]
     done = order[::-1][:phase]
     index = tuple(pl.ds(0, 4) if name in done else at[name] for name in DIMS)
-    return (at["c"],) + index + (slice(None), pl.ds(start, width))
-
-
-def plane_cut(plane, part, half=None):
-    ys = slice(None) if half is None else slice(half * 2, half * 2 + 2)
-    return (0, part, ys) if plane == 0 else (1, slice(None), part, ys)
+    return index + (slice(None), pl.ds(start, width))
+
+
+def plane_cut(plane, part, ys):
+    return (part, ys) if plane == 0 else (slice(None), part, ys)
 
 
 class Layer:
-    def __init__(self, number, me, sibling, x_ref, gain_ref, refs):
-        self.number, self.me, self.sibling, self.x, self.gain = number, me, sibling, x_ref, gain_ref
+    def __init__(self, me, x_ref, gain_ref, refs):
+        self.me, self.x, self.gain = me, x_ref, gain_ref
+        self.full, self.partial, self.acc, self.square, *lists = refs
         (
-            self.full, self.partial, self.core_in, self.acc, self.square,
-            *lists, self.gather_s, self.gather_r, self.pair_s, self.pair_r, self.core_s, self.core_r, self.sum_s, self.sum_r,
-        ) = refs
-        self.in1, self.held2, self.in2, self.held3, self.in3 = [lists[i * 3 : i * 3 + 3] for i in range(5)]
+            self.plane_s, self.plane_r, self.slab_s, self.slab_r, self.sum_s, self.sum_r, self.last_s, self.last_r
+        ) = lists[9:]
+        self.in1, self.held2, self.in2 = [lists[i * 3 : i * 3 + 3] for i in range(3)]
         self.ring = {name: [moved(me, **{name: step}) for step in (1, 2, 3)] for name in DIMS}
         self.back = {name: [moved(me, **{name: 4 - step}) for step in (1, 2, 3)] for name in DIMS}
         self.sends = []
@@ -256,100 +257,49 @@
         start, width, order = PORTIONS[p]
         me = self.me
         lanes = pl.ds(start, width)
-        scaled = self.x[:, lanes] * self.gain[pl.ds(f_me, 1), lanes]
-        self.full[me["c"], me["z"], me["y"], me["x"], :, lanes] = scaled.astype(BF16)
-        self.send(p, 0)
-
-    def send(self, p, phase):
-        axis = PORTIONS[p][2][2 - phase]
-        region = self.full.at[region_of(self.me, p, phase)]
-        for k in range(3):
-            copy = remote(
-                region, region, self.gather_s.at[p, phase, k], self.gather_r.at[p, phase, k], straight(self.ring[axis][k])
-            )
+        scaled = self.x[:, lanes] * self.gain[:, pl.ds(pl.multiple_of(f_me * BLK + start, 128), width)]
+        self.full[me["z"], me["y"], me["x"], :, lanes] = scaled.astype(BF16)
+        region = self.full.at[region_of(me, p, 0)]
+        for k, step in enumerate(PLANE):
+            to = straight(moved(me, **dict(zip(order[1:], step))))
+            copy = remote(region, region, self.plane_s.at[p, k], self.plane_r.at[p, k], to)
             copy.start()
             self.sends.append(copy)
 
-    def take(self, p, phase, k):
-        axis = PORTIONS[p][2][2 - phase]
-        region = self.full.at[region_of(self.back[axis][k], p, phase)]
-        remote(
-            region, region, self.gather_s.at[p, phase, k], self.gather_r.at[p, phase, k], straight(self.ring[axis][k])
-        ).wait_recv()
-        return region
-
-    def pair(self, p, k, plane):
-        place = self.me if k == 3 else self.back[PORTIONS[p][2][0]][k]
-        region = self.full.at[region_of(dict(place, c=plane), p, 2)]
-        return remote(region, region, self.pair_s.at[p, k], self.pair_r.at[p, k], self.sibling)
-
-    def spread(self):
-        for phase in (1, 2):
-            for p in range(3):
-                for k in range(3):
-                    self.take(p, phase - 1, k)
-                self.send(p, phase)
-                if phase == 2:
-                    self.pair(p, 3, self.me["c"]).start()
-
-    def forward(self):
+    def gather(self):
+        me = self.me
+        for p in range(3):
+            start, width, order = PORTIONS[p]
+            for k, step in enumerate(PLANE):
+                there = moved(me, **{name: 4 - by for name, by in zip(order[1:], step)})
+                region = self.full.at[region_of(there, p, 0)]
+                remote(region, region, self.plane_s.at[p, k], self.plane_r.at[p, k], straight(me)).wait_recv()
+            region = self.full.at[region_of(me, p, 2)]
+            for k in range(3):
+                to = straight(self.ring[order[0]][k])
+                copy = remote(region, region, self.slab_s.at[p, k], self.slab_r.at[p, k], to)
+                copy.start()
+                self.sends.append(copy)
         for k in (0, 2, 1):
             for p in range(3):
-                self.take(p, 2, k)
-                self.pair(p, k, self.me["c"]).start()
-
-    def take_pair(self, plane):
-        other = turned(self.sibling_real)
-        for k in (3, 0, 2, 1):
-            for p in range(3):
                 axis = PORTIONS[p][2][0]
-                place = other if k == 3 else moved(other, **{axis: 3 - k})
-                region = self.full.at[region_of(dict(place, c=plane), p, 2)]
-                remote(region, region, self.pair_s.at[p, k], self.pair_r.at[p, k], self.sibling).wait_recv()
-
-    def core_copy(self, plane, part):
-        cut = plane_cut(plane, part)
-        return remote(
-            self.partial.at[cut], self.core_in.at[cut[1:]], self.core_s.at[part], self.core_r.at[part], self.sibling
-        )
-
-    def core_sum(self, plane):
-        for part in range(4):
-            self.core_copy(plane, part).wait_recv()
-
-            def add(row, carry, part=part):
-                cut = (0, part, row) if plane == 0 else (1, row, part)
-                both = self.partial[cut].astype(F32) + self.core_in[cut[1:]].astype(F32)
-                self.partial[cut] = both.astype(BF16)
-                return carry
-
-            lax.fori_loop(0, 4, add, 0)
-
-    def start(self, p, phase, source):
-        axis = PORTIONS[p][2][phase]
-        into = (self.in1, self.in2, self.in3)[phase][p]
+                region = self.full.at[region_of(self.back[axis][k], p, 2)]
+                remote(region, region, self.slab_s.at[p, k], self.slab_r.at[p, k], straight(me)).wait_recv()
+
+    def first_sums(self, p):
+        begin, width, order = PORTIONS[p]
         copies = []
         for k in range(3):
-            to = self.ring[axis][k]
-            copy = remote(
-                source(to[axis]), into.at[k], self.sum_s.at[p, phase, k], self.sum_r.at[p, phase, k], straight(to)
-            )
-            copies.append(copy)
+            to = self.ring[order[0]][k]
+            index = [slice(None)] * 3
+            index[DIMS.index(order[0])] = to[order[0]]
+            source = self.partial.at[tuple(index) + (slice(None), pl.ds(begin, width))]
+            copies.append(remote(source, self.in1[p].at[k], self.sum_s.at[p, k], self.sum_r.at[p, k], straight(to)))
         return copies
-
-    def first_sums(self, p):
-        begin, width, order = PORTIONS[p]
-
-        def source(target):
-            index = [slice(None)] * 3
-            index[DIMS.index(order[0])] = target
-            return self.partial.at[(self.me["c"],) + tuple(index) + (slice(None), pl.ds(begin, width))]
-
-        return self.start(p, 0, source)
 
     def sums(self, finish):
         me = self.me
-        second, third = [], []
+        second = []
         for p in range(3):
             begin, width, order = PORTIONS[p]
             for copy in self.first_sums(p):
@@ -358,7 +308,7 @@
 
             def add(i, carry, p=p, begin=begin, width=width, order=order, left=left):
                 index = {order[0]: me[order[0]], left[0]: i, left[1]: slice(None)}
-                index = (me["c"],) + tuple(index[name] for name in DIMS) + (slice(None), pl.ds(begin, width))
+                index = tuple(index[name] for name in DIMS) + (slice(None), pl.ds(begin, width))
                 value = self.partial[index].astype(F32)
                 for k in range(3):
                     value = value + self.in1[p][k, i].astype(F32)
@@ -366,100 +316,66 @@
                 return carry
 
             lax.fori_loop(0, 4, add, 0)
-            if order[1] == left[0]:
-                second.append(self.start(p, 1, lambda target, p=p: self.held2[p].at[target]))
-            else:
-                second.append(self.start(p, 1, lambda target, p=p: self.held2[p].at[:, target]))
-            for copy in second[p]:
+            copies = []
+            for k, step in enumerate(PLANE):
+                to = moved(me, **dict(zip(left, step)))
+                source = self.held2[p].at[to[left[0]], to[left[1]]]
+                copy = remote(source, self.in2[p].at[k], self.last_s.at[p, k], self.last_r.at[p, k], straight(to))
                 copy.start()
+                copies.append(copy)
+            second.append(copies)
         for p in range(3):
             begin, width, order = PORTIONS[p]
             for copy in second[p]:
                 copy.wait_recv()
             left = [name for name in DIMS if name != order[0]]
-            mine = me[order[1]]
-            value = self.held2[p][mine] if order[1] == left[0] else self.held2[p][:, mine]
-            value = value.astype(F32)
-            for k in range(3):
-                value = value + self.in2[p][k].astype(F32)
-            self.held3[p][...] = value.astype(BF16)
-            third.append(self.start(p, 2, lambda target, p=p: self.held3[p].at[target]))
-            for copy in third[p]:
+            value = self.held2[p][me[left[0]], me[left[1]]].astype(F32)
+            value = value + jnp.sum(self.in2[p][...].astype(F32), axis=0)
+            finish(p, begin, width, value + self.x[:, begin : begin + width])
+            self.sends += second[p]
+
+    def run(self, multiply, activate, down, weights):
+        self.gather()
+        for wait in weights:
+            wait()
+        for plane in (0, 1):
+
+            @pl.when(self.me["c"] == plane)
+            def _(plane=plane):
+                self.acc[...] = jnp.zeros_like(self.acc)
+                self.square[...] = jnp.zeros_like(self.square)
+
+                def step(f, carry):
+                    rows = self.full[plane_cut(plane, f // 2, pl.ds((f % 2) * 2, 2))].reshape(128, BLK)
+                    at = pl.ds(pl.multiple_of(f * BLK, 128), BLK)
+                    multiply(rows, at)
+                    plain = rows.astype(F32) * (1.0 / self.gain[:, at])
+                    plain = plain * plain
+                    piece = plain[:, 0:128]
+                    for k in range(1, 7):
+                        piece = piece + plain[:, k * 128 : (k + 1) * 128]
+                    self.square[...] += piece
+                    return carry
+
+                lax.fori_loop(0, 8, step, 0)
+                scale = lax.rsqrt(jnp.sum(self.square[...], axis=1, keepdims=True) * (1.0 / D) + EPSILON)
+                act = activate(plane, scale)
+                for f in range(8):
+                    block = down(act, f).astype(BF16)
+                    shape = (2, 4, 16, BLK) if plane == 0 else (4, 2, 16, BLK)
+                    ys = slice(f % 2 * 2, f % 2 * 2 + 2)
+                    self.partial[plane_cut(plane, f // 2, ys)] = block.reshape(shape)
+
+        for p in range(3):
+            for copy in self.first_sums(p):
                 copy.start()
-        for p in range(3):
-            begin, width, order = PORTIONS[p]
-            for copy in third[p]:
-                copy.wait_recv()
-            value = self.held3[p][me[order[2]]].astype(F32)
-            for k in range(3):
-                value = value + self.in3[p][k].astype(F32)
-            finish(p, begin, width, value + self.x[:, begin : begin + width])
-        self.sends += second[0] + second[1] + second[2] + third[0] + third[1] + third[2]
-
-    def run(self, multiply, activate, down):
-        c = self.me["c"]
-        self.spread()
-        for plane in (0, 1):
-
-            @pl.when(c == plane)
-            def _():
-                self.forward()
-
-            @pl.when(c != plane)
-            def _(plane=plane):
-                self.take_pair(plane)
-
-            self.acc[...] = jnp.zeros_like(self.acc)
-            self.square[...] = jnp.zeros_like(self.square)
-
-            def step(f, carry, plane=plane):
-                part, ys = f // 2, pl.ds((f % 2) * 2, 2)
-                rows = self.full[0, part, ys] if plane == 0 else self.full[1, :, part, ys]
-                rows = rows.reshape(128, BLK)
-                multiply(rows, pl.ds(pl.multiple_of(f * BLK, 128), BLK))
-                plain = rows.astype(F32) * (1.0 / self.gain[pl.ds(f, 1), :])
-                plain = plain * plain
-                piece = plain[:, 0:128]
-                for k in range(1, 7):
-                    piece = piece + plain[:, k * 128 : (k + 1) * 128]
-                self.square[...] += piece
-                return carry
-
-            lax.fori_loop(0, 8, step, 0)
-            scale = lax.rsqrt(jnp.sum(self.square[...], axis=1, keepdims=True) * (1.0 / D) + EPSILON)
-            act = activate(plane, scale)
-            for part in range(4):
-                for half in range(2):
-                    block = down(act, part * 2 + half).astype(BF16)
-                    shape = (2, 4, 16, BLK) if plane == 0 else (4, 2, 16, BLK)
-                    self.partial[plane_cut(plane, part, half)] = block.reshape(shape)
-
-                @pl.when(c != plane)
-                def _(plane=plane, part=part):
-                    self.core_copy(plane, part).start()
-
-            @pl.when(c == plane)
-            def _(plane=plane):
-                self.core_sum(plane)
-                for p in range(3):
-                    for copy in self.first_sums(p):
-                        copy.start()
 
     def end(self):
-        c = self.me["c"]
         for copy in self.sends:
             copy.wait_send()
         for p in range(3):
-            for k in range(4):
-                self.pair(p, k, c).wait_send()
             for copy in self.first_sums(p):
                 copy.wait_send()
-        for plane in (0, 1):
-
-            @pl.when(c != plane)
-            def _(plane=plane):
-                for part in range(4):
-                    self.core_copy(plane, part).wait_send()
 
 
 def silu(value):
@@ -468,54 +384,65 @@
 
 def ffn_kernel(
     x_ref, gain1_ref, gain2_ref, wr_ref, chosen_ref, wg1_hbm, wu1_hbm, wd1_hbm, wg2_hbm, wu2_hbm, wd2_hbm, out_ref,
-    wg1, wu1, wd1, wg2, wu2, wd2, mid, router_acc, own, final_in, load_sem, final_s, final_r, *refs,
+    up1, down1, up2, down2, mid, router_acc, own, final_in, load_sem, give_s, give_r, final_s, final_r, *refs,
 ):
     here = coords()
     f_me = here["z"] * 2 + here["y"] // 2
     yh = here["y"] // 2
     me = turned(here)
     sibling = moved(here, c=1)
-    pairs = ((wg1_hbm, wg1), (wu1_hbm, wu1), (wd1_hbm, wd1), (wg2_hbm, wg2), (wu2_hbm, wu2), (wd2_hbm, wd2))
-    loads = [pltpu.make_async_copy(src, dst, load_sem.at[i]) for i, (src, dst) in enumerate(pairs)]
+    n1, n2 = wd1_hbm.shape[0], wd2_hbm.shape[0]
+    sources = (wg1_hbm, wu1_hbm, wd1_hbm, wg2_hbm, wu2_hbm, wd2_hbm)
+
+    def places(k):
+        return (
+            up1.at[pl.ds(k * n1, n1), :], up1.at[pl.ds(UP_AT + k * n1, n1), :], down1.at[pl.ds(k * n1, n1), :],
+            up2.at[k], up2.at[2 + k], down2.at[pl.ds(k * n2, n2), :],
+        )
+
+    loads = [pltpu.make_async_copy(src, dst, load_sem.at[i]) for i, (src, dst) in enumerate(zip(sources, places(0)))]
+    gives = [
+        remote(src, dst, give_s.at[i], give_r.at[i], sibling) for i, (src, dst) in enumerate(zip(sources, places(1)))
+    ]
     for load in loads:
         load.start()
     half = len(refs) // 2
-    dense = Layer(0, me, sibling, x_ref, gain1_ref, refs[:half])
-    routed = Layer(1, me, sibling, mid, gain2_ref, refs[half:])
-    dense.sibling_real = routed.sibling_real = sibling
+    dense = Layer(me, x_ref, gain1_ref, refs[:half])
+    routed = Layer(me, mid, gain2_ref, refs[half:])
     final_steps = [(dz, dy) for dy in (0, 2) for dz in range(4) if dz or dy]
     final_to = [moved(here, z=dz, y=dy) for dz, dy in final_steps]
     partners = [moved(here, **{name: step}) for name in DIMS for step in (1, 2, 3)] + [sibling]
-    meet(partners + [moved(here, z=dz, y=2) for dz in (1, 2, 3)])
+    for one, two in (("x", "y"), ("y", "z"), ("z", "x")):
+        partners += [moved(here, **{one: i, two: j}) for i in (1, 2, 3) for j in (1, 2, 3)]
+    meet(partners)
 
     for p in range(3):
         dense.begin(p, f_me)
-    for load in loads[:3]:
-        load.wait()
+    for give in gives:
+        give.start()
+    for first in (2 * n1, UP_AT + 2 * n1):
+        up1[first : first + UP_AT - 2 * n1, :] = jnp.zeros((UP_AT - 2 * n1, D), BF16)
 
     def multiply_dense(rows, at):
-        dense.acc[0] += dot_nt(rows, wg1[:, at])
-        dense.acc[1] += dot_nt(rows, wu1[:, at])
+        dense.acc[...] += dot_nt(rows, up1[:, at])
 
     def activate_dense(plane, scale):
-        return (silu(dense.acc[0] * scale) * (dense.acc[1] * scale)).astype(BF16)
+        gate, up = dense.acc[:, 0 : 2 * n1], dense.acc[:, UP_AT : UP_AT + 2 * n1]
+        return (silu(gate * scale) * (up * scale)).astype(BF16)
 
     def down_dense(act, f):
-        return dot(act, wd1[:, f * BLK : (f + 1) * BLK])
-
-    dense.run(multiply_dense, activate_dense, down_dense)
+        return dot(act, down1[:, f * BLK : (f + 1) * BLK])
+
+    dense.run(multiply_dense, activate_dense, down_dense, [q.wait for q in loads[:3]] + [q.wait_recv for q in gives[:3]])
 
     def between(p, begin, width, value):
         mid[:, begin : begin + width] = value
         routed.begin(p, f_me)
 
     dense.sums(between)
-    for load in loads[3:]:
-        load.wait()
-
     def multiply_routed(rows, at):
-        routed.acc[0] += dot(rows, wg2[at, :])
-        routed.acc[1] += dot(rows, wu2[at, :])
+        for k in range(4):
+            routed.acc[:, k * n2 : (k + 1) * n2] += dot(rows, up2[k, at, :])
         router_acc[...] += dot_nt(rows, wr_ref[:, at])
 
     def activate_routed(plane, scale):
@@ -527,14 +454,14 @@
         mine = lax.broadcasted_iota(jnp.int32, (128, 16), 1) == here["z"] * 4 + here["y"]
         weight = ROUTE_SCALE * jnp.sum(jnp.where(mine, picked, 0.0), axis=1, keepdims=True) / below
         wanted = jnp.sum(jnp.where(mine, chosen, 0.0), axis=1, keepdims=True) > 0.5
-        act = silu(routed.acc[0] * scale) * (routed.acc[1] * scale)
+        act = silu(routed.acc[:, : 2 * n2] * scale) * (routed.acc[:, 2 * n2 :] * scale)
         return jnp.where(wanted, act * weight, 0.0).astype(BF16)
 
     def down_routed(act, f):
-        return dot(act, wd2[:, f * BLK : (f + 1) * BLK])
+        return dot(act, down2[:, f * BLK : (f + 1) * BLK])
 
     router_acc[...] = jnp.zeros_like(router_acc)
-    routed.run(multiply_routed, activate_routed, down_routed)
+    routed.run(multiply_routed, activate_routed, down_routed, [q.wait for q in loads[3:]] + [q.wait_recv for q in gives[3:]])
 
     def last(p, begin, width, value):
         own[:, begin : begin + width] = value.astype(BF16)
@@ -552,36 +479,30 @@
     row = lax.broadcasted_iota(jnp.int32, (16, BLK), 0)
     for f in range(8):
         block = final_in[f // 2, f % 2].astype(F32)
-        for t in range(2):
-            out_ref[t : t + 1, f * BLK : (f + 1) * BLK] = jnp.sum(
-                jnp.where(row == f_me * 2 + t, block, 0.0), axis=0, keepdims=True
-            )
+        both = [jnp.sum(jnp.where(row == f_me * 2 + t, block, 0.0), axis=0, keepdims=True) for t in range(2)]
+        out_ref[:, f * BLK : (f + 1) * BLK] = jnp.concatenate(both, axis=0).astype(BF16)
     for copy in final_copies:
         copy.wait_send()
+    for give in gives:
+        give.wait_send()
     dense.end()
     routed.end()
 
 
-def layer_scratch(hidden):
+def layer_scratch(columns):
     dma = pltpu.SemaphoreType.DMA
     widths = [width for _, width, _ in PORTIONS]
     return (
         [
-            pltpu.VMEM((2, 4, 4, 4, 16, BLK), BF16),
-            pltpu.VMEM((2, 4, 4, 4, 16, BLK), BF16),
             pltpu.VMEM((4, 4, 4, 16, BLK), BF16),
-            pltpu.VMEM((2, 128, hidden), F32),
+            pltpu.VMEM((4, 4, 4, 16, BLK), BF16),
+            pltpu.VMEM((128, columns), F32),
             pltpu.VMEM((128, 128), F32),
         ]
         + [pltpu.VMEM((3, 4, 4, 16, width), BF16) for width in widths]
         + [pltpu.VMEM((4, 4, 16, width), BF16) for width in widths]
-        + [pltpu.VMEM((3, 4, 16, width), BF16) for width in widths]
-        + [pltpu.VMEM((4, 16, width), BF16) for width in widths]
-        + [pltpu.VMEM((3, 16, width), BF16) for width in widths]
-        + [
-            dma((3, 3, 3)), dma((3, 3, 3)), dma((3, 4)), dma((3, 4)),
-            dma((4,)), dma((4,)), dma((3, 3, 3)), dma((3, 3, 3)),
-        ]
+        + [pltpu.VMEM((15, 16, width), BF16) for width in widths]
+        + [dma((3, 15)), dma((3, 15)), dma((3, 3)), dma((3, 3)), dma((3, 3)), dma((3, 3)), dma((3, 15)), dma((3, 15))]
     )
 
 
@@ -589,21 +510,25 @@
     any_space = pl.BlockSpec(memory_space=pl.ANY)
     vmem = pl.BlockSpec(memory_space=pltpu.VMEM)
     dma = pltpu.SemaphoreType.DMA
+    n1, n2 = dense[2].shape[0], expert[2].shape[0]
     return pl.pallas_call(
         ffn_kernel,
-        out_shape=jax.ShapeDtypeStruct((2, D), F32),
+        out_shape=jax.ShapeDtypeStruct((2, D), BF16),
         in_specs=[vmem] * 5 + [any_space] * 6,
         out_specs=vmem,
-        scratch_shapes=[pltpu.VMEM(w.shape, BF16) for w in dense + expert]
-        + [
+        scratch_shapes=[
+            pltpu.VMEM((2 * UP_AT, D), BF16),
+            pltpu.VMEM((2 * n1, D), BF16),
+            pltpu.VMEM((4, D, n2), BF16),
+            pltpu.VMEM((2 * n2, D), BF16),
             pltpu.VMEM((16, BLK), F32),
             pltpu.VMEM((128, 16), F32),
             pltpu.VMEM((16, BLK), BF16),
             pltpu.VMEM((4, 2, 16, BLK), BF16),
-            dma((6,)), dma((7,)), dma((7,)),
+            dma((6,)), dma((6,)), dma((6,)), dma((7,)), dma((7,)),
         ]
-        + layer_scratch(dense[2].shape[0])
-        + layer_scratch(expert[2].shape[0]),
+        + layer_scratch(2 * UP_AT)
+        + layer_scratch(4 * n2),
         compiler_params=pltpu.CompilerParams(collective_id=1, has_side_effects=True, vmem_limit_bytes=VMEM_LIMIT),
         name="feed_forwards",
     )(shard, gain1, gain2, w_router, chosen, *dense, *expert)
@@ -661,14 +586,14 @@
     )
     out = feed_forwards(
         after_attn,
-        gain_attn.reshape(8, BLK),
-        gain_moe.reshape(8, BLK),
+        gain_attn.reshape(1, D),
+        gain_moe.reshape(1, D),
         w_router.T,
         chosen,
         (w_dense_gate.T, w_dense_up.T, w_dense_down),
         (w_expert_gate[0], w_expert_up[0], w_expert_down[0]),
     )
-    return out.astype(BF16)
+    return out
 
 
 def solution(mesh):

time: 148 us -> 132 us (0.89)
  the two profiles are of different devices: /device:TPU:1 before, /device:TPU:0 now
where the time goes in v3:
time: 132 us
  Pallas kernels  123 us (93%)
  matrix products  4.96 us (4%)
  local copies, waits for them, and re-layouts  2.34 us (2%)
  other arithmetic  1.76 us (1%)
    pallas_call x1, Pallas kernels, feed_forwards(): pl.pallas_call(ffn_kernel, out_shape=jax.ShapeDtypeStruct((2, D), BF16),...  88 us
    pallas_call x1, Pallas kernels, attn_exchange(): pl.pallas_call(attn_kernel, out_shape=(jax.ShapeDtypeStruct((16, BLK), F3...  34.8 us

profile of v3, /device:TPU:0, one launch (start us, length us, event | category | flops | bytes accessed | tf_op | source)
XLA Modules:
  0.0 131.9 jit_solution(7726171566109239405)
XLA Ops:
  0.0 0.0 copy-start
  0.0 1.0 copy-done
  1.0 0.8 fusion.12
  1.8 0.7 iota_compare_fusion
  2.5 0.7 slice_convert_fusion
  3.2 0.0 copy-start.1
  3.2 2.6 %fusion.16 = (f32[2,128]{1,0:T(2,128)S(1)}, f32[2,128,1024]{2,1,0:T(8,128)S(1)}) fusion(bf16[2,128,576]{1,2,0:T(8,128)(2,1)S(1)} %copy-done, bf16[2,1024,576]{1,2,0:T(8,128)(2,1)} %param.19, pred[2,1024]{1,0:T(4,128)(4,1)S(1)} %iota_compare_fusion), kind=kOutput, calls=%fused_computation.20 | convolution fusion | flops 302776064 | bytes 3705856 | tf_op jit(solution)/shard_map/thc,tlc->thl/dot_general | solution.py:540
  5.8 0.3 fusion.9
  6.1 0.0 copy-done.1
  6.2 1.6 %fusion.6 = bf16[2,128,512]{2,1,0:T(8,128)(2,1)} fusion(bf16[2,1024,576]{1,2,0:T(8,128)(2,1)S(1)} %copy-done.1, f32[2,128,1024]{2,1,0:T(8,128)S(1)} %get-tuple-element.12, f32[2,128]{1,0:T(2,128)S(1)} %get-tuple-element.10, f32[2,128]{1,0:T(2,128)S(1)} %multiply_maximum_fusion, f32[2,512]{1,0:T(2,128)S(1)} %slice_convert_fusion, ...), kind=kOutput, calls=%fused_computation.5 | convolution fusion | flops 269615104 | bytes 3415040 | tf_op jit(solution)/shard_map/thl,tlc->thc/dot_general | solution.py:555
  7.7 34.8 %attn_exchange.1 = (f32[16,896]{1,0:T(8,128)}, bf16[256,128]{1,0:T(8,128)(2,1)}) custom-call(bf16[2,8,16,512]{3,2,1,0:T(8,128)(2,1)} %bitcast.22, bf16[2,7168]{1,0:T(2,128)(2,1)} %hid_ref.1, s32[2,8]{1,0:T(2,128)} %ids_ref.1, bf16[16,512,128]{2,1,0:T(8,128)(2,1)} %wv_hbm.1, bf16[16,448,128]{2,1,0:T(8,128)(2,1)} %bitcast.21), custom_call_target="tpu_custom_call" | custom-call | tf_op jit(solution)/shard_map/attn_exchange/pallas_call | solution.py:194
  42.5 88.0 %feed_forwards.1 = bf16[2,7168]{1,0:T(2,128)(2,1)} custom-call(f32[16,896]{1,0:T(8,128)} %get-tuple-element.7.x_ref, f32[1,7168]{1,0:T(1,128)} %bitcast.24, f32[1,7168]{1,0:T(1,128)} %bitcast.25, bf16[16,7168]{1,0:T(8,128)(2,1)} %bitcast.23, bf16[256,128]{1,0:T(8,128)(2,1)} %get-tuple-element.8.chosen_ref, bf16[144,7168]{1,0:T(8,128)(2,1)} %bitcast.19, ...), custom_call_target="tpu_custom_call" | custom-call | tf_op jit(solution)/shard_map/feed_forwards/pallas_call | solution.py:514
  130.5 1.4 %copy.25 = bf16[2,7168]{1,0:T(2,128)(2,1)} copy(bf16[2,7168]{1,0:T(2,128)(2,1)} %feed_forwards.1) | data formatting | bytes 57344
  (2 shorter events, 0.0 us)
Async XLA Ops:
  0.0 1.0 copy-start
  3.2 2.9 %copy-start.1 = (bf16[2,1024,576]{1,2,0:T(8,128)(2,1)S(1)}, bf16[2,1024,576]{1,2,0:T(8,128)(2,1)}, u32[]{:S(2)}) copy-start(bf16[2,1024,576]{1,2,0:T(8,128)(2,1)} %param.19) | copy-start | bytes 7077892

commit v4 on v3

--- a/solution.py
+++ b/solution.py
@@ -39,11 +39,14 @@
     return new
 
 
-def meet(partners):
+def greet(partners):
     barrier = pltpu.get_barrier_semaphore()
     for partner in partners:
         pl.semaphore_signal(barrier, inc=1, device_id=device(partner), device_id_type=MESH)
-    pl.semaphore_wait(barrier, len(partners))
+
+
+def gathered(partners):
+    pl.semaphore_wait(pltpu.get_barrier_semaphore(), len(partners))
 
 
 def remote(src, dst, send, recv, partner):
@@ -60,21 +63,40 @@
     return jnp.dot(a, b, preferred_element_type=F32)
 
 
-def attn_kernel(
-    ctx_ref, hid_ref, ids_ref, wv_hbm, wo_hbm, out_ref, chosen_ref,
-    wv, wo, ctx_in, heads, part, part_in, hid_out, hid_in, mask_out, mask_in, load_sem,
-    hid_s, hid_r, ctx_s, ctx_r, mask_s, mask_r, hv_s, hv_r, part_s, part_r,
-):
-    me = coords()
+def attend(t, q, cache, latent, length):
+    scale = (VD + ROPE) ** (-0.5)
+    scores = lax.dot_general(q[t], cache[t], (((0,), (0,)), ((), ())), preferred_element_type=F32) * scale
+    own = lax.dot_general(q[t], latent, (((0,), (1,)), ((), ())), preferred_element_type=F32) * scale
+    own = own[:, t : t + 1]
+    place = lax.broadcasted_iota(jnp.int32, scores.shape, 1)
+    scores = jnp.where(place < length, scores, -jnp.inf)
+    peak = jnp.maximum(jnp.max(scores, axis=1, keepdims=True), own)
+    weights = jnp.exp(scores - peak)
+    own_weight = jnp.exp(own - peak)
+    total = jnp.sum(weights, axis=1, keepdims=True) + own_weight
+    probability = (weights / total).astype(BF16)
+    own_probability = (own_weight / total).astype(BF16).astype(F32)
+    context = dot_nt(probability, cache[t, 0:512, :])
+    return (context + own_probability * latent[t : t + 1, 0:512].astype(F32)).astype(BF16)
+
+
+def attention_part(me, len_ref, nl_ref, hid_ref, ids_ref, wv_hbm, wo_hbm, q_hbm, cache_hbm, shard, chosen_all, refs, meeting, early):
+    (
+        q, cache, latent, ctx, wv, wo, ctx_in, heads, part, part_in, hid_out, hid_in, mask_out, mask_in, load_sem,
+        hid_s, hid_r, ctx_s, ctx_r, mask_s, mask_r, hv_s, hv_r, hw_s, hw_r, part_s, part_r,
+    ) = refs
     x, c, z, y = me["x"], me["c"], me["z"], me["y"]
     yh, yl = y // 2, y % 2
     tp = x * 2 + c
     pad = pl.multiple_of(yl * 64, 64)
-    load_wv = pltpu.make_async_copy(wv_hbm, wv, load_sem.at[0])
-    load_wo = pltpu.make_async_copy(wo_hbm, wo.at[:, pl.ds(pad, 448), :], load_sem.at[1])
-    load_wv.start()
-    load_wo.start()
-    wo[:, pl.ds(pl.multiple_of((1 - yl) * 448, 64), 64), :] = jnp.zeros((16, 64, 128), BF16)
+    requests = []
+    for t in range(2):
+        pairs = ((q_hbm.at[t], q.at[t]), (cache_hbm.at[t], cache.at[t]))
+        requests.append([pltpu.make_async_copy(src, dst, load_sem.at[t * 2 + k]) for k, (src, dst) in enumerate(pairs)])
+    load_wv = pltpu.make_async_copy(wv_hbm, wv, load_sem.at[4])
+    load_wo = pltpu.make_async_copy(wo_hbm, wo.at[:, pl.ds(pad, 448), :], load_sem.at[5])
+    for load in requests[0] + requests[1] + [load_wv, load_wo]:
+        load.start()
 
     def at_tp(step):
         other = lax.rem(tp + step, 8)
@@ -84,8 +106,15 @@
     part_to = [dict(at_tp(dt), y=yh * 2 + (yl + dy) % 2) for dt, dy in tp_steps]
     hid_steps = [(dz, dy) for dy in (0, 2) for dz in range(4) if dz or dy]
     hid_to = [moved(me, z=dz, y=dy) for dz, dy in hid_steps]
-    other_odd = dict(me, y=lax.rem(yh * 2 + 2, 4) + (1 - yl))
-    meet(part_to + hid_to + [other_odd])
+    greet(meeting)
+    wo[:, pl.ds(pl.multiple_of((1 - yl) * 448, 64), 64), :] = jnp.zeros((16, 64, 128), BF16)
+    latent[...] = jnp.zeros_like(latent)
+    latent[0:2, :] = nl_ref[...].astype(F32)
+    latents = latent[...].astype(BF16)
+    for t in range(2):
+        for load in requests[t]:
+            load.wait()
+        ctx[t] = attend(t, q, cache, latents, len_ref[t]).reshape(8, 16, 512)
 
     first = (z * 2 + yh) * 2
     row = lax.broadcasted_iota(jnp.int32, (16, BLK), 0)
@@ -100,10 +129,11 @@
     row = lax.broadcasted_iota(jnp.int32, (16, 128), 0)
     placed = jnp.where(row == tp * 2, chosen[0:1, :], jnp.where(row == tp * 2 + 1, chosen[1:2, :], 0.0))
     mask_out[...] = placed.astype(BF16)
+    gathered(meeting)
     ctx_copies = []
     for step in range(1, 8):
         to = at_tp(step)
-        copy = remote(ctx_ref.at[:, to["x"] * 2 + to["c"]], ctx_in.at[tp], ctx_s.at[step - 1], ctx_r.at[step - 1], to)
+        copy = remote(ctx.at[:, to["x"] * 2 + to["c"]], ctx_in.at[tp], ctx_s.at[step - 1], ctx_r.at[step - 1], to)
         copy.start()
         ctx_copies.append(copy)
     for step in range(1, 8):
@@ -115,49 +145,60 @@
         copy = remote(hid_out.at[to["z"], to["y"] // 2], hid_in.at[z, yh], hid_s.at[i], hid_r.at[i], to)
         copy.start()
         hid_copies.append(copy)
-    ctx_in[tp] = ctx_ref[:, tp]
+    ctx_in[tp] = ctx[:, tp]
     mask_in[tp] = mask_out[...]
     hid_in[z, yh] = hid_out[z, yh]
     for copy in ctx_copies:
         copy.wait_recv()
     load_wv.wait()
+    early()
 
     i = lax.broadcasted_iota(jnp.int32, (256, 256), 0)
     j = lax.broadcasted_iota(jnp.int32, (256, 256), 1)
     turn = ((i & 15) * 16 + (i >> 4) == j).astype(BF16)
     by_head = dot(turn, ctx_in[...].reshape(256, 512)).astype(BF16)
-    for h in range(16):
-        heads[z, y, :, h * 128 : (h + 1) * 128] = dot(by_head[h * 16 : (h + 1) * 16, :], wv[h]).astype(BF16)
-
-    heads[z, y, :, 2048:2176] = jnp.sum(mask_in[...].astype(F32), axis=0).astype(BF16)
-
     halves = ((0, "z", "y"), (1, "y", "z"))
     sends = []
+
+    def lanes_of(half):
+        return pl.ds(half * 1024, 1024 + half * 128)
+
     for half, one, two in halves:
-        lanes = pl.ds(half * 1024, 1024 + half * 128)
-        for step in range(1, 4):
-            mine = heads.at[z, y, :, lanes]
-            copy = remote(mine, mine, hv_s.at[half, 0, step - 1], hv_r.at[half, 0, step - 1], moved(me, **{one: step}))
-            copy.start()
-            sends.append(copy)
+        for h in range(half * 8, half * 8 + 8):
+            heads[z, y, :, h * 128 : (h + 1) * 128] = dot(by_head[h * 16 : (h + 1) * 16, :], wv[h]).astype(BF16)
+        if half:
+            heads[z, y, :, 2048:2176] = jnp.sum(mask_in[...].astype(F32), axis=0).astype(BF16)
+        mine = heads.at[z, y, :, lanes_of(half)]
+        for k in (2, 1, 3):
+            to = moved(me, **{one: k})
+            sends.append(remote(mine, mine, hv_s.at[half, k - 1], hv_r.at[half, k - 1], to))
+            sends[-1].start()
+        for k in (2, 1, 3):
+            to = moved(me, **{two: k})
+            sends.append(remote(mine, mine, hw_s.at[half, 0, k - 1], hw_r.at[half, 0, k - 1], to))
+            sends[-1].start()
+    for k in (1, 3, 2):
+        for half, one, two in halves:
+            there = moved(me, **{one: 4 - k})
+            piece = heads.at[there["z"], there["y"], :, lanes_of(half)]
+            remote(piece, piece, hv_s.at[half, k - 1], hv_r.at[half, k - 1], me).wait_recv()
+            for hop in (2, 1, 3):
+                to = moved(me, **{two: hop})
+                sends.append(remote(piece, piece, hw_s.at[half, k, hop - 1], hw_r.at[half, k, hop - 1], to))
+                sends[-1].start()
+    load_wo.wait()
+
+    total = jnp.zeros((256, 512), F32)
     for half, one, two in halves:
-        lanes = pl.ds(half * 1024, 1024 + half * 128)
-        for step in range(1, 4):
-            sends[half * 3 + step - 1].wait_recv()
-        for step in range(1, 4):
-            slab = heads.at[:, y, :, lanes] if two == "y" else heads.at[z, :, :, lanes]
-            copy = remote(slab, slab, hv_s.at[half, 1, step - 1], hv_r.at[half, 1, step - 1], moved(me, **{two: step}))
-            copy.start()
-            sends.append(copy)
-    load_wo.wait()
-    for copy in sends[6:]:
-        copy.wait_recv()
-
-    total = jnp.zeros((256, 512), F32)
-    for pair in range(8):
-        rows = heads[:, :, :, pair * 256 : (pair + 1) * 256].reshape(256, 256)
-        weights = jnp.concatenate([wo[2 * pair], wo[2 * pair + 1]], axis=1)
-        total = total + dot_nt(rows, weights)
+        for k in range(4):
+            for hop in (1, 3, 2):
+                there = moved(me, **{one: (4 - k) % 4, two: 4 - hop})
+                piece = heads.at[there["z"], there["y"], :, lanes_of(half)]
+                remote(piece, piece, hw_s.at[half, k, hop - 1], hw_r.at[half, k, hop - 1], me).wait_recv()
+        for pair in range(half * 4, half * 4 + 4):
+            rows = heads[:, :, :, pair * 256 : (pair + 1) * 256].reshape(256, 256)
+            weights = jnp.concatenate([wo[2 * pair], wo[2 * pair + 1]], axis=1)
+            total = total + dot_nt(rows, weights)
     t, from_yh, from_z = i & 1, (i >> 1) & 1, (i >> 2) & 3
     source = from_z * 64 + (from_yh * 2 + (i >> 7)) * 16 + ((i >> 4) & 7) * 2 + t
     order = (source == j).astype(BF16)
@@ -174,46 +215,39 @@
     to_yl = ((i >> 6) & 1) * (1 - plane) + ((i >> 4) & 1) * plane
     to_x = ((i >> 4) & 3) * (1 - plane) + ((i >> 5) & 3) * plane
     source = from_z * 64 + (from_yh * 2 + to_yl) * 16 + to_x * 4 + plane * 2 + t
-    chosen_ref[...] = dot((source == j).astype(BF16), heads[:, :, :, 2048:2176].reshape(256, 128)).astype(BF16)
+    chosen_all[...] = dot((source == j).astype(BF16), heads[:, :, :, 2048:2176].reshape(256, 128)).astype(BF16)
     for copy in hid_copies:
         copy.wait_recv()
-    out_ref[...] = jnp.sum(hid_in[...].astype(F32), axis=(0, 1))
+    shard[...] = jnp.sum(hid_in[...].astype(F32), axis=(0, 1))
     for copy in part_copies:
         copy.wait_recv()
     sums = jnp.sum(part_in[...].astype(F32), axis=1)
-    out_ref[:, 0:512] += sums[0]
-    out_ref[:, 384:896] += sums[1]
-    for copy in ctx_copies + hid_copies + sends + part_copies:
-        copy.wait_send()
-
-
-def attn_exchange(context, hidden, ids, w_values, w_out):
-    any_space = pl.BlockSpec(memory_space=pl.ANY)
-    vmem = pl.BlockSpec(memory_space=pltpu.VMEM)
+    shard[:, 0:512] += sums[0]
+    shard[:, 384:896] += sums[1]
+    return ctx_copies + hid_copies + sends + part_copies
+
+
+def attention_scratch():
     dma = pltpu.SemaphoreType.DMA
-    return pl.pallas_call(
-        attn_kernel,
-        out_shape=(jax.ShapeDtypeStruct((16, BLK), F32), jax.ShapeDtypeStruct((256, 128), BF16)),
-        in_specs=[vmem, vmem, vmem, any_space, any_space],
-        out_specs=(vmem, vmem),
-        scratch_shapes=[
-            pltpu.VMEM((16, 512, 128), BF16),
-            pltpu.VMEM((16, 512, 128), BF16),
-            pltpu.VMEM((8, 2, 16, 512), BF16),
-            pltpu.VMEM((4, 4, 16, 2176), BF16),
-            pltpu.VMEM((2, 8, 16, 512), BF16),
-            pltpu.VMEM((2, 8, 16, 512), BF16),
-            pltpu.VMEM((4, 2, 16, BLK), BF16),
-            pltpu.VMEM((4, 2, 16, BLK), BF16),
-            pltpu.VMEM((16, 128), BF16),
-            pltpu.VMEM((8, 16, 128), BF16),
-            dma((2,)),
-            dma((7,)), dma((7,)), dma((7,)), dma((7,)), dma((7,)), dma((7,)),
-            dma((2, 2, 3)), dma((2, 2, 3)), dma((15,)), dma((15,)),
-        ],
-        compiler_params=pltpu.CompilerParams(collective_id=0, has_side_effects=True, vmem_limit_bytes=VMEM_LIMIT),
-        name="attn_exchange",
-    )(context, hidden, ids, w_values, w_out)
+    return [
+        pltpu.VMEM((2, 576, 128), BF16),
+        pltpu.VMEM((2, 576, 1024), BF16),
+        pltpu.VMEM((16, 576), F32),
+        pltpu.VMEM((2, 8, 16, 512), BF16),
+        pltpu.VMEM((16, 512, 128), BF16),
+        pltpu.VMEM((16, 512, 128), BF16),
+        pltpu.VMEM((8, 2, 16, 512), BF16),
+        pltpu.VMEM((4, 4, 16, 2176), BF16),
+        pltpu.VMEM((2, 8, 16, 512), BF16),
+        pltpu.VMEM((2, 8, 16, 512), BF16),
+        pltpu.VMEM((4, 2, 16, BLK), BF16),
+        pltpu.VMEM((4, 2, 16, BLK), BF16),
+        pltpu.VMEM((16, 128), BF16),
+        pltpu.VMEM((8, 16, 128), BF16),
+        dma((6,)),
+        dma((7,)), dma((7,)), dma((7,)), dma((7,)), dma((7,)), dma((7,)),
+        dma((2, 3)), dma((2, 3)), dma((2, 4, 3)), dma((2, 4, 3)), dma((15,)), dma((15,)),
+    ]
 
 
 def turned(at):
@@ -235,6 +269,12 @@
     done = order[::-1][:phase]
     index = tuple(pl.ds(0, 4) if name in done else at[name] for name in DIMS)
     return index + (slice(None), pl.ds(start, width))
+
+
+def portion_cut(plane, part, ys, p):
+    start, width, order = PORTIONS[p]
+    place = (part, ys, slice(None)) if plane == 0 else (slice(None), part, ys)
+    return place + (slice(None), pl.ds(start, width))
 
 
 def plane_cut(plane, part, ys):
@@ -360,15 +400,15 @@
                 lax.fori_loop(0, 8, step, 0)
                 scale = lax.rsqrt(jnp.sum(self.square[...], axis=1, keepdims=True) * (1.0 / D) + EPSILON)
                 act = activate(plane, scale)
-                for f in range(8):
-                    block = down(act, f).astype(BF16)
-                    shape = (2, 4, 16, BLK) if plane == 0 else (4, 2, 16, BLK)
-                    ys = slice(f % 2 * 2, f % 2 * 2 + 2)
-                    self.partial[plane_cut(plane, f // 2, ys)] = block.reshape(shape)
-
-        for p in range(3):
-            for copy in self.first_sums(p):
-                copy.start()
+                for p in range(3):
+                    start, width, order = PORTIONS[p]
+                    for f in range(8):
+                        block = down(act, slice(f * BLK + start, f * BLK + start + width)).astype(BF16)
+                        shape = (2, 4, 16, width) if plane == 0 else (4, 2, 16, width)
+                        ys = slice(f % 2 * 2, f % 2 * 2 + 2)
+                        self.partial[portion_cut(plane, f // 2, ys, p)] = block.reshape(shape)
+                    for copy in self.first_sums(p):
+                        copy.start()
 
     def end(self):
         for copy in self.sends:
@@ -382,9 +422,11 @@
     return value / (1.0 + jnp.exp(-value))
 
 
-def ffn_kernel(
-    x_ref, gain1_ref, gain2_ref, wr_ref, chosen_ref, wg1_hbm, wu1_hbm, wd1_hbm, wg2_hbm, wu2_hbm, wd2_hbm, out_ref,
-    up1, down1, up2, down2, mid, router_acc, own, final_in, load_sem, give_s, give_r, final_s, final_r, *refs,
+def layer_kernel(
+    len_ref, nl_ref, hid_ref, ids_ref, gain1_ref, gain2_ref, wr_ref, q_hbm, cache_hbm, wv_hbm, wo_hbm,
+    wg1_hbm, wu1_hbm, wd1_hbm, wg2_hbm, wu2_hbm, wd2_hbm, out_ref,
+    up1, down1, up2, down2, x_ref, chosen_ref, mid, router_acc, own, final_in, load_sem, give_s, give_r, final_s, final_r,
+    *refs,
 ):
     here = coords()
     f_me = here["z"] * 2 + here["y"] // 2
@@ -404,8 +446,8 @@
     gives = [
         remote(src, dst, give_s.at[i], give_r.at[i], sibling) for i, (src, dst) in enumerate(zip(sources, places(1)))
     ]
-    for load in loads:
-        load.start()
+    count = len(attention_scratch())
+    attention_refs, refs = refs[:count], refs[count:]
     half = len(refs) // 2
     dense = Layer(me, x_ref, gain1_ref, refs[:half])
     routed = Layer(me, mid, gain2_ref, refs[half:])
@@ -414,11 +456,23 @@
     partners = [moved(here, **{name: step}) for name in DIMS for step in (1, 2, 3)] + [sibling]
     for one, two in (("x", "y"), ("y", "z"), ("z", "x")):
         partners += [moved(here, **{one: i, two: j}) for i in (1, 2, 3) for j in (1, 2, 3)]
-    meet(partners)
-
+    partners += [moved(here, x=i, c=1) for i in (1, 2, 3)]
+    across = dict(here, y=yh * 2 + (1 - here["y"] % 2), c=1 - here["c"])
+    partners += [moved(across, x=i) for i in range(4)]
+
+    def early():
+        for load in loads:
+            load.start()
+        for give in gives[:3]:
+            give.start()
+
+    sent = attention_part(
+        here, len_ref, nl_ref, hid_ref, ids_ref, wv_hbm, wo_hbm, q_hbm, cache_hbm, x_ref, chosen_ref, attention_refs,
+        partners, early,
+    )
     for p in range(3):
         dense.begin(p, f_me)
-    for give in gives:
+    for give in gives[3:]:
         give.start()
     for first in (2 * n1, UP_AT + 2 * n1):
         up1[first : first + UP_AT - 2 * n1, :] = jnp.zeros((UP_AT - 2 * n1, D), BF16)
@@ -430,8 +484,8 @@
         gate, up = dense.acc[:, 0 : 2 * n1], dense.acc[:, UP_AT : UP_AT + 2 * n1]
         return (silu(gate * scale) * (up * scale)).astype(BF16)
 
-    def down_dense(act, f):
-        return dot(act, down1[:, f * BLK : (f + 1) * BLK])
+    def down_dense(act, at):
+        return dot(act, down1[:, at])
 
     dense.run(multiply_dense, activate_dense, down_dense, [q.wait for q in loads[:3]] + [q.wait_recv for q in gives[:3]])
 
@@ -457,8 +511,8 @@
         act = silu(routed.acc[:, : 2 * n2] * scale) * (routed.acc[:, 2 * n2 :] * scale)
         return jnp.where(wanted, act * weight, 0.0).astype(BF16)
 
-    def down_routed(act, f):
-        return dot(act, down2[:, f * BLK : (f + 1) * BLK])
+    def down_routed(act, at):
+        return dot(act, down2[:, at])
 
     router_acc[...] = jnp.zeros_like(router_acc)
     routed.run(multiply_routed, activate_routed, down_routed, [q.wait for q in loads[3:]] + [q.wait_recv for q in gives[3:]])
@@ -485,6 +539,8 @@
         copy.wait_send()
     for give in gives:
         give.wait_send()
+    for copy in sent:
+        copy.wait_send()
     dense.end()
     routed.end()
 
@@ -506,15 +562,15 @@
     )
 
 
-def feed_forwards(shard, gain1, gain2, w_router, chosen, dense, expert):
+def layer(lengths, latent, hidden, ids, gain1, gain2, w_router, queries, cache, w_values, w_out, dense, expert):
     any_space = pl.BlockSpec(memory_space=pl.ANY)
     vmem = pl.BlockSpec(memory_space=pltpu.VMEM)
     dma = pltpu.SemaphoreType.DMA
     n1, n2 = dense[2].shape[0], expert[2].shape[0]
     return pl.pallas_call(
-        ffn_kernel,
+        layer_kernel,
         out_shape=jax.ShapeDtypeStruct((2, D), BF16),
-        in_specs=[vmem] * 5 + [any_space] * 6,
+        in_specs=[pl.BlockSpec(memory_space=pltpu.SMEM)] + [vmem] * 6 + [any_space] * 10,
         out_specs=vmem,
         scratch_shapes=[
             pltpu.VMEM((2 * UP_AT, D), BF16),
@@ -522,43 +578,21 @@
             pltpu.VMEM((4, D, n2), BF16),
             pltpu.VMEM((2 * n2, D), BF16),
             pltpu.VMEM((16, BLK), F32),
+            pltpu.VMEM((256, 128), BF16),
+            pltpu.VMEM((16, BLK), F32),
             pltpu.VMEM((128, 16), F32),
             pltpu.VMEM((16, BLK), BF16),
             pltpu.VMEM((4, 2, 16, BLK), BF16),
             dma((6,)), dma((6,)), dma((6,)), dma((7,)), dma((7,)),
         ]
+        + attention_scratch()
         + layer_scratch(2 * UP_AT)
         + layer_scratch(4 * n2),
-        compiler_params=pltpu.CompilerParams(collective_id=1, has_side_effects=True, vmem_limit_bytes=VMEM_LIMIT),
-        name="feed_forwards",
-    )(shard, gain1, gain2, w_router, chosen, *dense, *expert)
-
-
-def latent_attention(queries, cache, new_latent, lengths, latent_dim):
-    score_scale = (VD + ROPE) ** (-0.5)
-    scores = (
-        jnp.einsum("thc,tlc->thl", queries, cache, preferred_element_type=jnp.float32) * score_scale
-    )
-    own_score = (
-        jnp.einsum("thc,tc->th", queries, new_latent, preferred_element_type=jnp.float32)
-        * score_scale
-    )
-    places = jnp.arange(cache.shape[1], dtype=jnp.int32)
-    in_range = places[None, None, :] < lengths[:, None, None]
-    scores = jnp.where(in_range, scores, -jnp.inf)
-    peak = jnp.maximum(jnp.max(scores, axis=2), own_score)
-    weights = jnp.exp(scores - peak[:, :, None])
-    own_weight = jnp.exp(own_score - peak)
-    sum_total = jnp.sum(weights, axis=2) + own_weight
-    probability = (weights / sum_total[:, :, None]).astype(jnp.bfloat16)
-    own_probability = (own_weight / sum_total).astype(jnp.bfloat16)
-    context = jnp.einsum(
-        "thl,tlc->thc", probability, cache[:, :, :latent_dim], preferred_element_type=jnp.float32
-    )
-    context = context + own_probability.astype(jnp.float32)[:, :, None] * new_latent[
-        :, None, :latent_dim
-    ].astype(jnp.float32)
-    return context.astype(jnp.bfloat16)
+        compiler_params=pltpu.CompilerParams(collective_id=0, has_side_effects=True, vmem_limit_bytes=VMEM_LIMIT),
+        name="decode_layer",
+    )(
+        lengths, latent, hidden, ids, gain1, gain2, w_router, queries, cache, w_values, w_out, *dense, *expert
+    )
 
 
 def body(
@@ -580,16 +614,18 @@
     w_expert_up,
     w_expert_down,
 ):
-    context = latent_attention(queries, cache, new_latent, lengths, w_values.shape[1])
-    after_attn, chosen = attn_exchange(
-        context.reshape(2, 8, 16, 512), hidden, expert_ids, w_values, jnp.swapaxes(w_out, 1, 2)
-    )
-    out = feed_forwards(
-        after_attn,
+    out = layer(
+        lengths,
+        new_latent,
+        hidden,
+        expert_ids,
         gain_attn.reshape(1, D),
         gain_moe.reshape(1, D),
         w_router.T,
-        chosen,
+        jnp.swapaxes(queries, 1, 2),
+        jnp.swapaxes(cache, 1, 2),
+        w_values,
+        jnp.swapaxes(w_out, 1, 2),
         (w_dense_gate.T, w_dense_up.T, w_dense_down),
         (w_expert_gate[0], w_expert_up[0], w_expert_down[0]),
     )

time: 132 us -> 119 us (0.902)
  Pallas kernels: 123 us -> 117 us
  matrix products: 4.96 us -> 0 us
  other arithmetic: 1.76 us -> 0 us
    pallas_call x2 -> x1, Pallas kernels: 123 us -> 117 us  [layer(): pl.pallas_call(layer_kernel, out_shape=jax.ShapeDtypeStruct((2, D), BF16)...]
    dot_general x3 -> x0, matrix products: 4.96 us -> none  [the longest x1 2.57 us: latent_attention(): jnp.einsum('thc,tlc->thl', queries, cache, preferred_element_type=jnp.flo...]
where the time goes in v4:
time: 119 us
  Pallas kernels  117 us (98%)
  local copies, waits for them, and re-layouts  1.38 us (1%)
    pallas_call x1, Pallas kernels, layer(): pl.pallas_call(layer_kernel, out_shape=jax.ShapeDtypeStruct((2, D), BF16)...  117 us

profile of v4, /device:TPU:0, one launch (start us, length us, event | category | flops | bytes accessed | tf_op | source)
XLA Modules:
  0.0 118.9 jit_solution(15091349711585128854)
XLA Ops:
  0.0 117.5 %decode_layer.1 = bf16[2,7168]{1,0:T(2,128)(2,1)} custom-call(s32[2]{0:T(128)} %len_ref.1, bf16[2,576]{1,0:T(2,128)(2,1)} %nl_ref.1, bf16[2,7168]{1,0:T(2,128)(2,1)} %hid_ref.1, s32[2,8]{1,0:T(2,128)} %ids_ref.1, f32[1,7168]{1,0:T(1,128)} %bitcast.20, f32[1,7168]{1,0:T(1,128)} %bitcast.21, bf16[16,7168]{1,0:T(8,128)(2,1)} %bitcast.19, ...), custom_call_target="tpu_custom_call" | custom-call | tf_op jit(solution)/shard_map/decode_layer/pallas_call | solution.py:570
  117.5 1.4 %copy.19 = bf16[2,7168]{1,0:T(2,128)(2,1)} copy(bf16[2,7168]{1,0:T(2,128)(2,1)} %decode_layer.1) | data formatting | bytes 57344

commit v5 on v4

--- a/solution.py
+++ b/solution.py
@@ -9,7 +9,6 @@
 VD = 128
 D = 7168
 BLK = 896
-UP_AT = 384
 EPSILON = 1e-06
 ROUTE_SCALE = 2.5
 MESH = pl.DeviceIdType.MESH
@@ -21,6 +20,8 @@
 PORTIONS = ((0, 384, ("x", "y", "z")), (384, 256, ("y", "z", "x")), (640, 256, ("z", "x", "y")))
 DIMS = ("z", "y", "x")
 PLANE = sorted(((i, j) for i in range(4) for j in range(4) if i or j), key=lambda d: -sum(min(k, 4 - k) for k in d))
+
+ROWS = (2, 1, 3, 0)
 
 
 def coords():
@@ -111,10 +112,19 @@
     latent[...] = jnp.zeros_like(latent)
     latent[0:2, :] = nl_ref[...].astype(F32)
     latents = latent[...].astype(BF16)
+    ctx_copies = []
     for t in range(2):
         for load in requests[t]:
             load.wait()
         ctx[t] = attend(t, q, cache, latents, len_ref[t]).reshape(8, 16, 512)
+        if t == 0:
+            gathered(meeting)
+        for step in (4, 3, 5, 2, 6, 1, 7):
+            to = at_tp(step)
+            source, into = ctx.at[t, to["x"] * 2 + to["c"]], ctx_in.at[tp, t]
+            copy = remote(source, into, ctx_s.at[t, step - 1], ctx_r.at[t, step - 1], to)
+            copy.start()
+            ctx_copies.append(copy)
 
     first = (z * 2 + yh) * 2
     row = lax.broadcasted_iota(jnp.int32, (16, BLK), 0)
@@ -129,13 +139,6 @@
     row = lax.broadcasted_iota(jnp.int32, (16, 128), 0)
     placed = jnp.where(row == tp * 2, chosen[0:1, :], jnp.where(row == tp * 2 + 1, chosen[1:2, :], 0.0))
     mask_out[...] = placed.astype(BF16)
-    gathered(meeting)
-    ctx_copies = []
-    for step in range(1, 8):
-        to = at_tp(step)
-        copy = remote(ctx.at[:, to["x"] * 2 + to["c"]], ctx_in.at[tp], ctx_s.at[step - 1], ctx_r.at[step - 1], to)
-        copy.start()
-        ctx_copies.append(copy)
     for step in range(1, 8):
         copy = remote(mask_out, mask_in.at[tp], mask_s.at[step - 1], mask_r.at[step - 1], at_tp(step))
         copy.start()
@@ -245,7 +248,7 @@
         pltpu.VMEM((16, 128), BF16),
         pltpu.VMEM((8, 16, 128), BF16),
         dma((6,)),
-        dma((7,)), dma((7,)), dma((7,)), dma((7,)), dma((7,)), dma((7,)),
+        dma((7,)), dma((7,)), dma((2, 7)), dma((2, 7)), dma((7,)), dma((7,)),
         dma((2, 3)), dma((2, 3)), dma((2, 4, 3)), dma((2, 4, 3)), dma((15,)), dma((15,)),
     ]
 
@@ -308,96 +311,97 @@
 
     def gather(self):
         me = self.me
-        for p in range(3):
-            start, width, order = PORTIONS[p]
-            for k, step in enumerate(PLANE):
-                there = moved(me, **{name: 4 - by for name, by in zip(order[1:], step)})
-                region = self.full.at[region_of(there, p, 0)]
-                remote(region, region, self.plane_s.at[p, k], self.plane_r.at[p, k], straight(me)).wait_recv()
-            region = self.full.at[region_of(me, p, 2)]
-            for k in range(3):
-                to = straight(self.ring[order[0]][k])
-                copy = remote(region, region, self.slab_s.at[p, k], self.slab_r.at[p, k], to)
-                copy.start()
-                self.sends.append(copy)
-        for k in (0, 2, 1):
+        for row in (0, 1, 3, 2):
             for p in range(3):
-                axis = PORTIONS[p][2][0]
-                region = self.full.at[region_of(self.back[axis][k], p, 2)]
-                remote(region, region, self.slab_s.at[p, k], self.slab_r.at[p, k], straight(me)).wait_recv()
-
-    def first_sums(self, p):
+                start, width, order = PORTIONS[p]
+                for k, step in enumerate(PLANE):
+                    if step[0] == row:
+                        there = moved(me, **{name: 4 - by for name, by in zip(order[1:], step)})
+                        region = self.full.at[region_of(there, p, 0)]
+                        remote(region, region, self.plane_s.at[p, k], self.plane_r.at[p, k], straight(me)).wait_recv()
+                region = self.full.at[region_of(moved(me, **{order[1]: 4 - row}), p, 1)]
+                for k in (1, 0, 2):
+                    to = straight(self.ring[order[0]][k])
+                    copy = remote(region, region, self.slab_s.at[p, row, k], self.slab_r.at[p, row, k], to)
+                    copy.start()
+                    self.sends.append(copy)
+
+    def take(self, p):
+        order = PORTIONS[p][2]
+        for row in (0, 1, 3, 2):
+            for k in (0, 2, 1):
+                there = moved(self.back[order[0]][k], **{order[1]: 4 - row})
+                region = self.full.at[region_of(there, p, 1)]
+                remote(region, region, self.slab_s.at[p, row, k], self.slab_r.at[p, row, k], straight(self.me)).wait_recv()
+
+    def first_sums(self, p, row):
         begin, width, order = PORTIONS[p]
+        left = [name for name in DIMS if name != order[0]]
+        there = moved(self.me, **{left[0]: row})
         copies = []
-        for k in range(3):
+        for k in (1, 0, 2):
             to = self.ring[order[0]][k]
-            index = [slice(None)] * 3
-            index[DIMS.index(order[0])] = to[order[0]]
-            source = self.partial.at[tuple(index) + (slice(None), pl.ds(begin, width))]
-            copies.append(remote(source, self.in1[p].at[k], self.sum_s.at[p, k], self.sum_r.at[p, k], straight(to)))
+            index = dict(there, **{order[0]: to[order[0]], left[1]: slice(None)})
+            source = self.partial.at[tuple(index[name] for name in DIMS) + (slice(None), pl.ds(begin, width))]
+            into = self.in1[p].at[k, there[left[0]]]
+            copies.append(remote(source, into, self.sum_s.at[p, row, k], self.sum_r.at[p, row, k], straight(to)))
         return copies
 
     def sums(self, finish):
         me = self.me
         second = []
+        for row in ROWS:
+            for p in range(3):
+                begin, width, order = PORTIONS[p]
+                for copy in self.first_sums(p, row):
+                    copy.wait_recv()
+                left = [name for name in DIMS if name != order[0]]
+                there = moved(me, **{left[0]: row})
+                index = dict(there, **{left[1]: slice(None)})
+                value = self.partial[tuple(index[name] for name in DIMS) + (slice(None), pl.ds(begin, width))].astype(F32)
+                for k in range(3):
+                    value = value + self.in1[p][k, there[left[0]]].astype(F32)
+                self.held2[p][there[left[0]]] = value.astype(BF16)
+                for k, step in enumerate(PLANE):
+                    if step[0] == row:
+                        to = moved(me, **dict(zip(left, step)))
+                        source = self.held2[p].at[to[left[0]], to[left[1]]]
+                        into = self.in2[p].at[k]
+                        copy = remote(source, into, self.last_s.at[p, k], self.last_r.at[p, k], straight(to))
+                        copy.start()
+                        second.append((p, copy))
         for p in range(3):
             begin, width, order = PORTIONS[p]
-            for copy in self.first_sums(p):
-                copy.wait_recv()
-            left = [name for name in DIMS if name != order[0]]
-
-            def add(i, carry, p=p, begin=begin, width=width, order=order, left=left):
-                index = {order[0]: me[order[0]], left[0]: i, left[1]: slice(None)}
-                index = tuple(index[name] for name in DIMS) + (slice(None), pl.ds(begin, width))
-                value = self.partial[index].astype(F32)
-                for k in range(3):
-                    value = value + self.in1[p][k, i].astype(F32)
-                self.held2[p][i] = value.astype(BF16)
-                return carry
-
-            lax.fori_loop(0, 4, add, 0)
-            copies = []
-            for k, step in enumerate(PLANE):
-                to = moved(me, **dict(zip(left, step)))
-                source = self.held2[p].at[to[left[0]], to[left[1]]]
-                copy = remote(source, self.in2[p].at[k], self.last_s.at[p, k], self.last_r.at[p, k], straight(to))
-                copy.start()
-                copies.append(copy)
-            second.append(copies)
-        for p in range(3):
-            begin, width, order = PORTIONS[p]
-            for copy in second[p]:
-                copy.wait_recv()
+            for at, copy in second:
+                if at == p:
+                    copy.wait_recv()
             left = [name for name in DIMS if name != order[0]]
             value = self.held2[p][me[left[0]], me[left[1]]].astype(F32)
             value = value + jnp.sum(self.in2[p][...].astype(F32), axis=0)
             finish(p, begin, width, value + self.x[:, begin : begin + width])
-            self.sends += second[p]
+        self.sends += [copy for at, copy in second]
 
     def run(self, multiply, activate, down, weights):
         self.gather()
+        for p in range(3):
+            self.take(p)
         for wait in weights:
             wait()
         for plane in (0, 1):
 
             @pl.when(self.me["c"] == plane)
             def _(plane=plane):
-                self.acc[...] = jnp.zeros_like(self.acc)
-                self.square[...] = jnp.zeros_like(self.square)
-
-                def step(f, carry):
-                    rows = self.full[plane_cut(plane, f // 2, pl.ds((f % 2) * 2, 2))].reshape(128, BLK)
-                    at = pl.ds(pl.multiple_of(f * BLK, 128), BLK)
-                    multiply(rows, at)
+                for f in range(8):
+                    rows = self.full[plane_cut(plane, f // 2, slice(f % 2 * 2, f % 2 * 2 + 2))].reshape(128, BLK)
+                    at = slice(f * BLK, (f + 1) * BLK)
+                    multiply(rows, at, f == 0)
                     plain = rows.astype(F32) * (1.0 / self.gain[:, at])
                     plain = plain * plain
                     piece = plain[:, 0:128]
                     for k in range(1, 7):
                         piece = piece + plain[:, k * 128 : (k + 1) * 128]
-                    self.square[...] += piece
-                    return carry
-
-                lax.fori_loop(0, 8, step, 0)
+                    put(self.square, piece, f == 0)
+
                 scale = lax.rsqrt(jnp.sum(self.square[...], axis=1, keepdims=True) * (1.0 / D) + EPSILON)
                 act = activate(plane, scale)
                 for p in range(3):
@@ -407,15 +411,24 @@
                         shape = (2, 4, 16, width) if plane == 0 else (4, 2, 16, width)
                         ys = slice(f % 2 * 2, f % 2 * 2 + 2)
                         self.partial[portion_cut(plane, f // 2, ys, p)] = block.reshape(shape)
-                    for copy in self.first_sums(p):
-                        copy.start()
+                    for row in ROWS:
+                        for copy in self.first_sums(p, row):
+                            copy.start()
 
     def end(self):
         for copy in self.sends:
             copy.wait_send()
         for p in range(3):
-            for copy in self.first_sums(p):
-                copy.wait_send()
+            for row in ROWS:
+                for copy in self.first_sums(p, row):
+                    copy.wait_send()
+
+
+def put(ref, value, first):
+    if first:
+        ref[...] = value
+    else:
+        ref[...] += value
 
 
 def silu(value):
@@ -438,7 +451,7 @@
 
     def places(k):
         return (
-            up1.at[pl.ds(k * n1, n1), :], up1.at[pl.ds(UP_AT + k * n1, n1), :], down1.at[pl.ds(k * n1, n1), :],
+            up1.at[pl.ds(k * n1, n1), :], up1.at[pl.ds((2 + k) * n1, n1), :], down1.at[pl.ds(k * n1, n1), :],
             up2.at[k], up2.at[2 + k], down2.at[pl.ds(k * n2, n2), :],
         )
 
@@ -474,14 +487,11 @@
         dense.begin(p, f_me)
     for give in gives[3:]:
         give.start()
-    for first in (2 * n1, UP_AT + 2 * n1):
-        up1[first : first + UP_AT - 2 * n1, :] = jnp.zeros((UP_AT - 2 * n1, D), BF16)
-
-    def multiply_dense(rows, at):
-        dense.acc[...] += dot_nt(rows, up1[:, at])
+    def multiply_dense(rows, at, first):
+        put(dense.acc, dot_nt(up1[:, at], rows), first)
 
     def activate_dense(plane, scale):
-        gate, up = dense.acc[:, 0 : 2 * n1], dense.acc[:, UP_AT : UP_AT + 2 * n1]
+        gate, up = dense.acc[0 : 2 * n1, :].T, dense.acc[2 * n1 :, :].T
         return (silu(gate * scale) * (up * scale)).astype(BF16)
 
     def down_dense(act, at):
@@ -494,14 +504,13 @@
         routed.begin(p, f_me)
 
     dense.sums(between)
-    def multiply_routed(rows, at):
+    def multiply_routed(rows, at, first):
         for k in range(4):
-            routed.acc[:, k * n2 : (k + 1) * n2] += dot(rows, up2[k, at, :])
-        router_acc[...] += dot_nt(rows, wr_ref[:, at])
+            put(routed.acc.at[:, k * n2 : (k + 1) * n2], dot(rows, up2[k, at, :]), first)
+        put(router_acc, dot_nt(rows, wr_ref[:, at]), first)
 
     def activate_routed(plane, scale):
         affinity = 1.0 / (1.0 + jnp.exp(-(router_acc[...] * scale)))
-        router_acc[...] = jnp.zeros_like(router_acc)
         chosen = chosen_ref[plane * 128 : plane * 128 + 128, 0:16].astype(F32)
         picked = jnp.where(chosen > 0.5, affinity, 0.0)
         below = jnp.sum(picked, axis=1, keepdims=True)
@@ -514,7 +523,6 @@
     def down_routed(act, at):
         return dot(act, down2[:, at])
 
-    router_acc[...] = jnp.zeros_like(router_acc)
     routed.run(multiply_routed, activate_routed, down_routed, [q.wait for q in loads[3:]] + [q.wait_recv for q in gives[3:]])
 
     def last(p, begin, width, value):
@@ -545,20 +553,20 @@
     routed.end()
 
 
-def layer_scratch(columns):
+def layer_scratch(products):
     dma = pltpu.SemaphoreType.DMA
     widths = [width for _, width, _ in PORTIONS]
     return (
         [
             pltpu.VMEM((4, 4, 4, 16, BLK), BF16),
             pltpu.VMEM((4, 4, 4, 16, BLK), BF16),
-            pltpu.VMEM((128, columns), F32),
+            pltpu.VMEM(products, F32),
             pltpu.VMEM((128, 128), F32),
         ]
         + [pltpu.VMEM((3, 4, 4, 16, width), BF16) for width in widths]
         + [pltpu.VMEM((4, 4, 16, width), BF16) for width in widths]
         + [pltpu.VMEM((15, 16, width), BF16) for width in widths]
-        + [dma((3, 15)), dma((3, 15)), dma((3, 3)), dma((3, 3)), dma((3, 3)), dma((3, 3)), dma((3, 15)), dma((3, 15))]
+        + [dma((3, 15)), dma((3, 15)), dma((3, 4, 3)), dma((3, 4, 3)), dma((3, 4, 3)), dma((3, 4, 3)), dma((3, 15)), dma((3, 15))]
     )
 
 
@@ -573,7 +581,7 @@
         in_specs=[pl.BlockSpec(memory_space=pltpu.SMEM)] + [vmem] * 6 + [any_space] * 10,
         out_specs=vmem,
         scratch_shapes=[
-            pltpu.VMEM((2 * UP_AT, D), BF16),
+            pltpu.VMEM((4 * n1, D), BF16),
             pltpu.VMEM((2 * n1, D), BF16),
             pltpu.VMEM((4, D, n2), BF16),
             pltpu.VMEM((2 * n2, D), BF16),
@@ -586,8 +594,8 @@
             dma((6,)), dma((6,)), dma((6,)), dma((7,)), dma((7,)),
         ]
         + attention_scratch()
-        + layer_scratch(2 * UP_AT)
-        + layer_scratch(4 * n2),
+        + layer_scratch((4 * n1, 128))
+        + layer_scratch((128, 4 * n2)),
         compiler_params=pltpu.CompilerParams(collective_id=0, has_side_effects=True, vmem_limit_bytes=VMEM_LIMIT),
         name="decode_layer",
     )(

time: 119 us -> 112 us (0.941)
  Pallas kernels: 117 us -> 111 us
    pallas_call x1, Pallas kernels: 117 us -> 111 us  [layer(): pl.pallas_call(layer_kernel, out_shape=jax.ShapeDtypeStruct((2, D), BF16)...]
where the time goes in v5:
time: 112 us
  Pallas kernels  111 us (99%)
  local copies, waits for them, and re-layouts  1.38 us (1%)
    pallas_call x1, Pallas kernels, layer(): pl.pallas_call(layer_kernel, out_shape=jax.ShapeDtypeStruct((2, D), BF16)...  111 us

profile of v5, /device:TPU:0, one launch (start us, length us, event | category | flops | bytes accessed | tf_op | source)
XLA Modules:
  0.0 112.1 jit_solution(8095464073403120407)
XLA Ops:
  0.0 110.7 %decode_layer.1 = bf16[2,7168]{1,0:T(2,128)(2,1)} custom-call(s32[2]{0:T(128)} %len_ref.1, bf16[2,576]{1,0:T(2,128)(2,1)} %nl_ref.1, bf16[2,7168]{1,0:T(2,128)(2,1)} %hid_ref.1, s32[2,8]{1,0:T(2,128)} %ids_ref.1, f32[1,7168]{1,0:T(1,128)} %bitcast.20, f32[1,7168]{1,0:T(1,128)} %bitcast.21, bf16[16,7168]{1,0:T(8,128)(2,1)} %bitcast.19, ...), custom_call_target="tpu_custom_call" | custom-call | tf_op jit(solution)/shard_map/decode_layer/pallas_call | solution.py:578
  110.7 1.4 %copy.19 = bf16[2,7168]{1,0:T(2,128)(2,1)} copy(bf16[2,7168]{1,0:T(2,128)(2,1)} %decode_layer.1) | data formatting | bytes 57344

commit v6 on v5

--- a/solution.py
+++ b/solution.py
@@ -22,6 +22,8 @@
 PLANE = sorted(((i, j) for i in range(4) for j in range(4) if i or j), key=lambda d: -sum(min(k, 4 - k) for k in d))
 
 ROWS = (2, 1, 3, 0)
+
+LAUNCH = [(k, p) for k in sorted(range(15), key=lambda k: (PLANE[k][0] != 0, k)) for p in range(3)]
 
 
 def coords():
@@ -103,7 +105,7 @@
         other = lax.rem(tp + step, 8)
         return dict(me, x=other // 2, c=other % 2)
 
-    tp_steps = [(dt, dy) for dy in (0, 1) for dt in range(8) if dt or dy]
+    tp_steps = [(dt, dy) for dy in (1, 0) for dt in (4, 5, 3, 2, 6, 7, 1, 0) if dt or dy]
     part_to = [dict(at_tp(dt), y=yh * 2 + (yl + dy) % 2) for dt, dy in tp_steps]
     hid_steps = [(dz, dy) for dy in (0, 2) for dz in range(4) if dz or dy]
     hid_to = [moved(me, z=dz, y=dy) for dz, dy in hid_steps]
@@ -302,15 +304,19 @@
         lanes = pl.ds(start, width)
         scaled = self.x[:, lanes] * self.gain[:, pl.ds(pl.multiple_of(f_me * BLK + start, 128), width)]
         self.full[me["z"], me["y"], me["x"], :, lanes] = scaled.astype(BF16)
-        region = self.full.at[region_of(me, p, 0)]
-        for k, step in enumerate(PLANE):
-            to = straight(moved(me, **dict(zip(order[1:], step))))
+
+    def launch(self):
+        for k, p in LAUNCH:
+            order = PORTIONS[p][2]
+            region = self.full.at[region_of(self.me, p, 0)]
+            to = straight(moved(self.me, **dict(zip(order[1:], PLANE[k]))))
             copy = remote(region, region, self.plane_s.at[p, k], self.plane_r.at[p, k], to)
             copy.start()
             self.sends.append(copy)
 
     def gather(self):
         me = self.me
+        self.launch()
         for row in (0, 1, 3, 2):
             for p in range(3):
                 start, width, order = PORTIONS[p]
@@ -438,7 +444,7 @@
 def layer_kernel(
     len_ref, nl_ref, hid_ref, ids_ref, gain1_ref, gain2_ref, wr_ref, q_hbm, cache_hbm, wv_hbm, wo_hbm,
     wg1_hbm, wu1_hbm, wd1_hbm, wg2_hbm, wu2_hbm, wd2_hbm, out_ref,
-    up1, down1, up2, down2, x_ref, chosen_ref, mid, router_acc, own, final_in, load_sem, give_s, give_r, final_s, final_r,
+    up1, down1, up2, down2, x_ref, chosen_ref, mid, router_acc, own, packed, final_in, load_sem, give_s, give_r, final_s, final_r,
     *refs,
 ):
     here = coords()
@@ -464,7 +470,7 @@
     half = len(refs) // 2
     dense = Layer(me, x_ref, gain1_ref, refs[:half])
     routed = Layer(me, mid, gain2_ref, refs[half:])
-    final_steps = [(dz, dy) for dy in (0, 2) for dz in range(4) if dz or dy]
+    final_steps = [(dz, dy) for dz in (2, 1, 3, 0) for dy in (2, 0) if dz or dy]
     final_to = [moved(here, z=dz, y=dy) for dz, dy in final_steps]
     partners = [moved(here, **{name: step}) for name in DIMS for step in (1, 2, 3)] + [sibling]
     for one, two in (("x", "y"), ("y", "z"), ("z", "x")):
@@ -530,18 +536,25 @@
 
     routed.sums(last)
 
+    tiles = [own[:, k * 128 : (k + 1) * 128] for k in range(7)] + [jnp.zeros((16, 128), BF16)]
+    i = lax.broadcasted_iota(jnp.int32, (128, 128), 0)
+    j = lax.broadcasted_iota(jnp.int32, (128, 128), 1)
+    spot = i & 15
+    token = (spot >= 7).astype(jnp.int32)
+    source = (spot - 7 * token) * 16 + (i >> 4) * 2 + token
+    pick = jnp.where(spot < 14, source, -1) == j
+    packed[...] = dot(pick.astype(BF16), jnp.concatenate(tiles, axis=0)).astype(BF16).reshape(4, 2, 16, 128)
     final_copies = []
     for i, to in enumerate(final_to):
-        copy = remote(own, final_in.at[here["z"], yh], final_s.at[i], final_r.at[i], to)
+        copy = remote(packed.at[to["z"], to["y"] // 2], final_in.at[here["z"], yh], final_s.at[i], final_r.at[i], to)
         copy.start()
         final_copies.append(copy)
-    final_in[here["z"], yh] = own[...]
+    final_in[here["z"], yh] = packed[here["z"], yh]
     for copy in final_copies:
         copy.wait_recv()
-    row = lax.broadcasted_iota(jnp.int32, (16, BLK), 0)
     for f in range(8):
         block = final_in[f // 2, f % 2].astype(F32)
-        both = [jnp.sum(jnp.where(row == f_me * 2 + t, block, 0.0), axis=0, keepdims=True) for t in range(2)]
+        both = [jnp.concatenate([block[t * 7 + k : t * 7 + k + 1, :] for k in range(7)], axis=1) for t in range(2)]
         out_ref[:, f * BLK : (f + 1) * BLK] = jnp.concatenate(both, axis=0).astype(BF16)
     for copy in final_copies:
         copy.wait_send()
@@ -590,7 +603,8 @@
             pltpu.VMEM((16, BLK), F32),
             pltpu.VMEM((128, 16), F32),
             pltpu.VMEM((16, BLK), BF16),
-            pltpu.VMEM((4, 2, 16, BLK), BF16),
+            pltpu.VMEM((4, 2, 16, 128), BF16),
+            pltpu.VMEM((4, 2, 16, 128), BF16),
             dma((6,)), dma((6,)), dma((6,)), dma((7,)), dma((7,)),
         ]
         + attention_scratch()

time: 112 us -> 110 us (0.982)
  Pallas kernels: 111 us -> 108 us
    pallas_call x1, Pallas kernels: 111 us -> 108 us  [layer(): pl.pallas_call(layer_kernel, out_shape=jax.ShapeDtypeStruct((2, D), BF16)...]
where the time goes in v6:
time: 110 us
  Pallas kernels  108 us (98%)
  local copies, waits for them, and re-layouts  1.38 us (1%)
    pallas_call x1, Pallas kernels, layer(): pl.pallas_call(layer_kernel, out_shape=jax.ShapeDtypeStruct((2, D), BF16)...  108 us

profile of v6, /device:TPU:0, one launch (start us, length us, event | category | flops | bytes accessed | tf_op | source)
XLA Modules:
  0.0 109.9 jit_solution(2911049710279282555)
XLA Ops:
  0.0 108.5 %decode_layer.1 = bf16[2,7168]{1,0:T(2,128)(2,1)} custom-call(s32[2]{0:T(128)} %len_ref.1, bf16[2,576]{1,0:T(2,128)(2,1)} %nl_ref.1, bf16[2,7168]{1,0:T(2,128)(2,1)} %hid_ref.1, s32[2,8]{1,0:T(2,128)} %ids_ref.1, f32[1,7168]{1,0:T(1,128)} %bitcast.20, f32[1,7168]{1,0:T(1,128)} %bitcast.21, bf16[16,7168]{1,0:T(8,128)(2,1)} %bitcast.19, ...), custom_call_target="tpu_custom_call" | custom-call | tf_op jit(solution)/shard_map/decode_layer/pallas_call | solution.py:591
  108.5 1.4 %copy.19 = bf16[2,7168]{1,0:T(2,128)(2,1)} copy(bf16[2,7168]{1,0:T(2,128)(2,1)} %decode_layer.1) | data formatting | bytes 57344

commit v7 on v6

--- a/solution.py
+++ b/solution.py
@@ -389,25 +389,33 @@
 
     def run(self, multiply, activate, down, weights):
         self.gather()
-        for p in range(3):
-            self.take(p)
         for wait in weights:
             wait()
+        for portions, start, width in (((1, 2), 384, 512), ((0,), 0, 384)):
+            for p in portions:
+                self.take(p)
+            for plane in (0, 1):
+
+                @pl.when(self.me["c"] == plane)
+                def _(plane=plane, start=start, width=width):
+                    for f in range(8):
+                        place = plane_cut(plane, f // 2, slice(f % 2 * 2, f % 2 * 2 + 2))
+                        place += (slice(None),) * (4 - len(place)) + (slice(start, start + width),)
+                        rows = self.full[place].reshape(128, width)
+                        at = slice(f * BLK + start, f * BLK + start + width)
+                        first = f == 0 and start > 0
+                        multiply(rows, at, first)
+                        plain = rows.astype(F32) * (1.0 / self.gain[:, at])
+                        plain = plain * plain
+                        piece = plain[:, 0:128]
+                        for k in range(1, width // 128):
+                            piece = piece + plain[:, k * 128 : (k + 1) * 128]
+                        put(self.square, piece, first)
+
         for plane in (0, 1):
 
             @pl.when(self.me["c"] == plane)
             def _(plane=plane):
-                for f in range(8):
-                    rows = self.full[plane_cut(plane, f // 2, slice(f % 2 * 2, f % 2 * 2 + 2))].reshape(128, BLK)
-                    at = slice(f * BLK, (f + 1) * BLK)
-                    multiply(rows, at, f == 0)
-                    plain = rows.astype(F32) * (1.0 / self.gain[:, at])
-                    plain = plain * plain
-                    piece = plain[:, 0:128]
-                    for k in range(1, 7):
-                        piece = piece + plain[:, k * 128 : (k + 1) * 128]
-                    put(self.square, piece, f == 0)
-
                 scale = lax.rsqrt(jnp.sum(self.square[...], axis=1, keepdims=True) * (1.0 / D) + EPSILON)
                 act = activate(plane, scale)
                 for p in range(3):

time: 110 us -> 108 us (0.982)
  Pallas kernels: 108 us -> 106 us
    pallas_call x1, Pallas kernels: 108 us -> 106 us  [layer(): pl.pallas_call(layer_kernel, out_shape=jax.ShapeDtypeStruct((2, D), BF16)...]
where the time goes in v7:
time: 108 us
  Pallas kernels  106 us (98%)
  local copies, waits for them, and re-layouts  1.38 us (1%)
    pallas_call x1, Pallas kernels, layer(): pl.pallas_call(layer_kernel, out_shape=jax.ShapeDtypeStruct((2, D), BF16)...  106 us

profile of v7, /device:TPU:0, one launch (start us, length us, event | category | flops | bytes accessed | tf_op | source)
XLA Modules:
  0.0 107.9 jit_solution(18167375289880802525)
XLA Ops:
  0.0 106.5 %decode_layer.1 = bf16[2,7168]{1,0:T(2,128)(2,1)} custom-call(s32[2]{0:T(128)} %len_ref.1, bf16[2,576]{1,0:T(2,128)(2,1)} %nl_ref.1, bf16[2,7168]{1,0:T(2,128)(2,1)} %hid_ref.1, s32[2,8]{1,0:T(2,128)} %ids_ref.1, f32[1,7168]{1,0:T(1,128)} %bitcast.20, f32[1,7168]{1,0:T(1,128)} %bitcast.21, bf16[16,7168]{1,0:T(8,128)(2,1)} %bitcast.19, ...), custom_call_target="tpu_custom_call" | custom-call | tf_op jit(solution)/shard_map/decode_layer/pallas_call | solution.py:599
  106.5 1.4 %copy.19 = bf16[2,7168]{1,0:T(2,128)(2,1)} copy(bf16[2,7168]{1,0:T(2,128)(2,1)} %decode_layer.1) | data formatting | bytes 57344
